TPU v7x, 32 devices: a whole 2x2x4 slice. The times are simulated.
32 devices in a mesh: shots: 2 (over x), xline: 8 (over z, y), inline: 2 (over core).
Axes of the slice: x: 2, y: 2, z: 4, core: 2. Of those that a mesh axis runs over, the one named last changes fastest.
Arguments:
- fwd_now: float32 [128, 64, 256], P(('shots', 'inline'), 'xline'), parts along dimension 0, may hold values from -6 to 6
- fwd_before: float32 [128, 64, 256], P(('shots', 'inline'), 'xline'), parts along dimension 0, may hold values from -6 to 6
- adj_now: float32 [128, 64, 256], P(('shots', 'inline'), 'xline'), parts along dimension 0, may hold values from -6 to 6
- adj_before: float32 [128, 64, 256], P(('shots', 'inline'), 'xline'), parts along dimension 0, may hold values from -6 to 6
- velocity: float32 [64, 64, 256], P('inline', 'xline'), may hold values from 0.2 to 0.4
- log_density: float32 [64, 64, 256], P('inline', 'xline'), may hold values from -0.3 to 0.3
- observed: float32 [16, 2048], P('shots', ('xline', 'inline')), parts along dimension 0, may hold values from -48 to 48
- rec_cells: int32 [16, 128], P(('xline', 'inline')), may hold values from 0 to 65535
- rec_counts: int32 [16, 16], P(('xline', 'inline')), may hold values from 0 to 8, as said below
- src_cell: int32 [32], P('shots'), parts along dimension 0, may hold values from 0 to 1048575
- wavelet: float32 [16, 16], P('shots'), parts along dimension 0, may hold values from -144 to 144
Outputs:
- gradient: float32 [512, 64, 64], P(('shots', 'xline'), 'inline'), parts along dimension 0
- adjoint_state: float32 [128, 64, 256], P(('shots', 'inline'), 'xline'), parts along dimension 0
- adjoint_previous: float32 [128, 64, 256], P(('shots', 'inline'), 'xline'), parts along dimension 0
There are 2 independent parts, one for each index of `shots`. A program takes and returns all parts, laid end to end along the dimension named above; an argument that names none is the same for every part. Nothing has to cross between parts.
Inputs may be any that keep to these rules, and one draw needn't show every extreme that they name: rec_counts[o, s] live slots of the 8 that device s sends to subdomain o; in every draw one subdomain receives 8 live slots from every device.
All inputs are finite; a program needn't handle non-finite values.
Results may differ from a plain program's by a relative error of at most 0.04.
Values sent between devices are 32-bit elements; how exact they have to be, the bound alone decides.
A program may use at most 64 MiB of HBM per device.

v0:
```python
import functools

import jax
import jax.numpy as jnp
from jax import lax
from jax.experimental import pallas as pl
from jax.experimental.pallas import tpu as pltpu
from jax.sharding import PartitionSpec as P

CAP = 8
SMOOTH = 16
MESH = pl.DeviceIdType.MESH

SECOND_COEFFS = (-205.0 / 72.0, 8.0 / 5.0, -1.0 / 5.0, 8.0 / 315.0, -1.0 / 560.0)
FIRST_COEFFS = (4.0 / 5.0, -1.0 / 5.0, 4.0 / 105.0, -1.0 / 280.0)
LEFT, RIGHT, UP, DOWN = 0, 1, 2, 3
DENSITY = 4


def split_bf16(value):
    high = value.astype(jnp.bfloat16)
    low = (value - high.astype(jnp.float32)).astype(jnp.bfloat16)
    return high, low


def dot(a, b):
    return jnp.dot(a, b, preferred_element_type=jnp.float32)


def wave_kernel(
    sizes,
    fwd_now, fwd_before, adj_now, adj_before, velocity, density,
    traces, rec_row, rec_row_t, rec_z, rec_live, src_row, src_z, wavelet,
    raw_out, last_out, previous_out,
    field, x_in, x_out, accel, base, image, slopes, speed_sq,
    row_map, row_map_t, z_map, z_high, z_low, residual_ref,
    send_sem, recv_sem,
):
    n_i, n_x, depth, steps, n_xline, n_inline = sizes
    rows = n_i * n_x
    xl = lax.axis_index("xline")
    core = lax.axis_index("inline")
    side = lax.rem(xl, 2)
    half = lax.rem(side + lax.rem(core, 2), 2)
    mate = xl + 1 - 2 * side
    has = (
        xl >= 2,
        xl < n_xline - 2,
        core * 2 + half > 0,
        core * 2 + half < 2 * n_inline - 1,
    )
    target = (
        {"xline": xl - 2},
        {"xline": xl + 2},
        {"xline": jnp.where(half == 1, mate, xl), "inline": jnp.where(half == 1, core, core - 1)},
        {"xline": jnp.where(half == 0, mate, xl), "inline": jnp.where(half == 0, core, core + 1)},
    )
    inner_x = pl.ds(8, n_x)

    def copy_of(idx, way):
        if way == LEFT:
            src, dst = x_out.at[idx, 0], x_in.at[idx, 1]
        elif way == RIGHT:
            src, dst = x_out.at[idx, 1], x_in.at[idx, 0]
        elif way == UP:
            src = field.at[idx, pl.ds(4, 4), inner_x, :]
            dst = field.at[idx, pl.ds(n_i + 4, 4), inner_x, :]
        else:
            src = field.at[idx, pl.ds(n_i, 4), inner_x, :]
            dst = field.at[idx, pl.ds(0, 4), inner_x, :]
        return pltpu.make_async_remote_copy(
            src_ref=src, dst_ref=dst,
            send_sem=send_sem.at[idx, way], recv_sem=recv_sem.at[idx, way],
            device_id=target[way], device_id_type=MESH,
        )

    def send(idx):
        x_out[idx, 0] = field[idx, pl.ds(4, n_i), pl.ds(8, 4), :]
        x_out[idx, 1] = field[idx, pl.ds(4, n_i), pl.ds(4 + n_x, 4), :]
        for way in range(4):
            @pl.when(has[way])
            def _():
                copy_of(idx, way).start()

    def finish(idx):
        for way in range(4):
            @pl.when(has[way])
            def _():
                copy_of(idx, way).wait_send()
                copy_of(idx, way ^ 1).wait_recv()
        field[idx, pl.ds(4, n_i), pl.ds(4, 4), :] = x_in[idx, 0]
        field[idx, pl.ds(4, n_i), pl.ds(8 + n_x, 4), :] = x_in[idx, 1]

    for idx in range(5):
        field[idx, pl.ds(0, 4)] = jnp.zeros((4,) + field.shape[2:], jnp.float32)
        field[idx, pl.ds(n_i + 4, 4)] = jnp.zeros((4,) + field.shape[2:], jnp.float32)
    x_in[...] = jnp.zeros(x_in.shape, jnp.float32)

    barrier = pltpu.get_barrier_semaphore()
    for way in range(4):
        @pl.when(has[way])
        def _():
            pl.semaphore_signal(barrier, inc=1, device_id=target[way], device_id_type=MESH)
    pl.semaphore_wait(barrier, sum(present.astype(jnp.int32) for present in has))

    inner_i = pl.ds(4, n_i)
    field[DENSITY, inner_i, inner_x, :] = density[...]
    field[0, inner_i, inner_x, :] = fwd_now[...]
    send(DENSITY)
    send(0)
    field[2, inner_i, inner_x, :] = adj_now[...]
    send(2)
    field[1, inner_i, inner_x, :] = fwd_before[...]
    field[3, inner_i, inner_x, :] = adj_before[...]

    speed_sq[...] = velocity[...] * velocity[...]
    image[...] = jnp.zeros(image.shape, jnp.float32)
    slots = rec_row.shape[0]
    row_map[...] = (lax.broadcasted_iota(jnp.int32, (rows, slots), 0) == rec_row_t[...]).astype(jnp.float32).astype(jnp.bfloat16)
    row_map_t[...] = (lax.broadcasted_iota(jnp.int32, (slots, rows), 1) == rec_row[...]).astype(jnp.float32).astype(jnp.bfloat16)
    z_map[...] = (lax.broadcasted_iota(jnp.int32, (slots, depth), 1) == rec_z[...]).astype(jnp.float32)
    src_rows = (lax.broadcasted_iota(jnp.int32, (rows, src_row.shape[1]), 0) == src_row[...]).astype(jnp.float32)
    src_cols = (lax.broadcasted_iota(jnp.int32, (src_z.shape[0], depth), 1) == src_z[...]).astype(jnp.float32).astype(jnp.bfloat16)
    offset = lax.broadcasted_iota(jnp.int32, (depth, depth), 0) - lax.broadcasted_iota(jnp.int32, (depth, depth), 1)
    second = jnp.where(offset == 0, 3.0 * SECOND_COEFFS[0], 0.0)
    first = jnp.zeros((depth, depth), jnp.float32)
    for k in range(1, 5):
        second = jnp.where((offset == k) | (offset == -k), SECOND_COEFFS[k], second)
        first = jnp.where(offset == k, FIRST_COEFFS[k - 1], first)
        first = jnp.where(offset == -k, -FIRST_COEFFS[k - 1], first)
    high, low = split_bf16(second)
    z_high[:, pl.ds(0, depth)] = high
    z_low[:, pl.ds(0, depth)] = low
    high, low = split_bf16(first)
    z_high[:, pl.ds(depth, depth)] = high
    z_low[:, pl.ds(depth, depth)] = low

    def flat(idx):
        return field[idx, inner_i, inner_x, :].reshape(rows, depth)

    def along_depth(idx):
        high, low = split_bf16(flat(idx))
        both = dot(high, z_high[...]) + (dot(low, z_high[...]) + dot(high, z_low[...]))
        return both[:, :depth], both[:, depth:]

    def across(idx, i):
        lap = slope_i = slope_x = None
        for k in range(1, 5):
            plus_i = field[idx, i + 4 + k, inner_x, :]
            minus_i = field[idx, i + 4 - k, inner_x, :]
            plus_x = field[idx, i + 4, pl.ds(8 + k, n_x), :]
            minus_x = field[idx, i + 4, pl.ds(8 - k, n_x), :]
            terms = (
                SECOND_COEFFS[k] * ((plus_i + minus_i) + (plus_x + minus_x)),
                FIRST_COEFFS[k - 1] * (plus_i - minus_i),
                FIRST_COEFFS[k - 1] * (plus_x - minus_x),
            )
            if lap is None:
                lap, slope_i, slope_x = terms
            else:
                lap, slope_i, slope_x = lap + terms[0], slope_i + terms[1], slope_x + terms[2]
        return lap, slope_i, slope_x

    def prepare(idx, term):
        lap, slope = along_depth(idx)
        partial = term + speed_sq[...].reshape(rows, depth) * (lap - slopes[2].reshape(rows, depth) * slope)
        base[...] = partial.reshape(n_i, n_x, depth)

    slopes[2] = along_depth(DENSITY)[1].reshape(n_i, n_x, depth)
    finish(DENSITY)

    @pl.loop(0, n_i)
    def _(i):
        _, slope_i, slope_x = across(DENSITY, i)
        slopes[0, i] = slope_i
        slopes[1, i] = slope_x

    @pl.loop(0, steps)
    def _(t):
        now = lax.rem(t, 2)
        other = 1 - now
        high, low = split_bf16(src_rows * wavelet[pl.ds(t, 1), :])
        prepare(now, dot(high, src_cols) + dot(low, src_cols))
        finish(now)

        @pl.loop(0, n_i)
        def _(i):
            lap, slope_i, slope_x = across(now, i)
            change = base[i] + speed_sq[i] * (lap - slopes[0, i] * slope_i - slopes[1, i] * slope_x)
            accel[t, i] = change
            field[other, i + 4, inner_x, :] = (
                2.0 * field[now, i + 4, inner_x, :] - field[other, i + 4, inner_x, :] + change
            )

        @pl.when(t < steps - 1)
        def _():
            send(other)

        high, low = split_bf16(flat(other))
        picked = dot(row_map_t[...], high) + dot(row_map_t[...], low)
        predicted = jnp.sum(picked * z_map[...], axis=1, keepdims=True)
        column = lax.broadcasted_iota(jnp.int32, traces.shape, 1) == t
        seen = jnp.sum(jnp.where(column, traces[...], 0.0), axis=1, keepdims=True)
        residual_ref[t] = rec_live[...] * (predicted - seen)

    @pl.loop(0, steps)
    def _(j):
        now = 2 + lax.rem(j, 2)
        other = 5 - now
        t = steps - 1 - j
        high, low = split_bf16(residual_ref[t] * z_map[...])
        prepare(now, dot(row_map[...], high) + dot(row_map[...], low))
        finish(now)

        @pl.loop(0, n_i)
        def _(i):
            lap, slope_i, slope_x = across(now, i)
            change = base[i] + speed_sq[i] * (lap - slopes[0, i] * slope_i - slopes[1, i] * slope_x)
            fresh = 2.0 * field[now, i + 4, inner_x, :] - field[other, i + 4, inner_x, :] + change
            field[other, i + 4, inner_x, :] = fresh
            image[i] += fresh * accel[t, i]

        @pl.when(j < steps - 1)
        def _():
            send(other)

    raw_out[...] = image[...] * (2.0 / steps) / velocity[...]
    last_out[...] = field[2 + steps % 2, inner_i, inner_x, :]
    previous_out[...] = field[2 + (steps - 1) % 2, inner_i, inner_x, :]


def per_device(
    fwd_now, fwd_before, adj_now, adj_before, velocity, log_density,
    observed, rec_cells, rec_counts, src_cell, wavelet,
):
    tile_i, tile_x, depth = fwd_now.shape
    steps = wavelet.shape[0]
    n_xline = lax.axis_size("xline")
    n_inline = lax.axis_size("inline")
    full_x = tile_x * n_xline
    n_i, n_x = tile_i // 2, tile_x * 2
    xl = lax.axis_index("xline")
    core = lax.axis_index("inline")
    side = xl % 2
    half = (side + core) % 2
    swap = [(k, k ^ 1) for k in range(n_xline)]

    def pair_up(mine, theirs, axis):
        return jnp.where(
            side == 0,
            jnp.concatenate([mine, theirs], axis=axis),
            jnp.concatenate([theirs, mine], axis=axis),
        )

    def gather_pair(value):
        kept = lax.dynamic_slice_in_dim(value, half * n_i, n_i, axis=0)
        sent = lax.dynamic_slice_in_dim(value, (1 - half) * n_i, n_i, axis=0)
        return pair_up(kept, lax.ppermute(sent, "xline", swap), 1)

    routed = lax.all_to_all(observed, ("xline", "inline"), split_axis=1, concat_axis=1, tiled=True)
    live = (jnp.arange(CAP)[None, :] < rec_counts[0][:, None]).astype(jnp.int32).reshape(1, -1)
    lists = jnp.concatenate([rec_cells, live], axis=0)
    lists = pair_up(lists, lax.ppermute(lists, "xline", swap), 1)
    traces = pair_up(routed, lax.ppermute(routed, "xline", swap), 1).T
    cells = lists[0]
    slots = cells.shape[0]
    cell_i = cells // (tile_x * depth) - half * n_i
    cell_x = cells // depth % tile_x + jnp.where(jnp.arange(slots) < slots // 2, 0, tile_x)
    rec_row = jnp.where((cell_i >= 0) & (cell_i < n_i), cell_i * n_x + cell_x, -1)
    rec_z = cells % depth
    src_i = src_cell // (full_x * depth) - (core * tile_i + half * n_i)
    src_x = src_cell // depth % full_x - (xl // 2) * n_x
    inside = (src_i >= 0) & (src_i < n_i) & (src_x >= 0) & (src_x < n_x)
    src_row = jnp.where(inside, src_i * n_x + src_x, -1)
    src_z = src_cell % depth

    block = (n_i, n_x, depth)
    rows = n_i * n_x
    vmem = pl.BlockSpec(memory_space=pltpu.VMEM)
    kernel = functools.partial(wave_kernel, (n_i, n_x, depth, steps, n_xline, n_inline))
    raw, last, previous = pl.pallas_call(
        kernel,
        out_shape=[jax.ShapeDtypeStruct(block, jnp.float32)] * 3,
        in_specs=[vmem] * 14,
        out_specs=[vmem] * 3,
        scratch_shapes=[
            pltpu.VMEM((5, n_i + 8, n_x + 16, depth), jnp.float32),
            pltpu.VMEM((5, 2, n_i, 4, depth), jnp.float32),
            pltpu.VMEM((5, 2, n_i, 4, depth), jnp.float32),
            pltpu.VMEM((steps,) + block, jnp.float32),
            pltpu.VMEM(block, jnp.float32),
            pltpu.VMEM(block, jnp.float32),
            pltpu.VMEM((3,) + block, jnp.float32),
            pltpu.VMEM(block, jnp.float32),
            pltpu.VMEM((rows, slots), jnp.bfloat16),
            pltpu.VMEM((slots, rows), jnp.bfloat16),
            pltpu.VMEM((slots, depth), jnp.float32),
            pltpu.VMEM((depth, 2 * depth), jnp.bfloat16),
            pltpu.VMEM((depth, 2 * depth), jnp.bfloat16),
            pltpu.VMEM((steps, slots, 1), jnp.float32),
            pltpu.SemaphoreType.DMA((5, 4)),
            pltpu.SemaphoreType.DMA((5, 4)),
        ],
        compiler_params=pltpu.CompilerParams(
            collective_id=0, has_side_effects=True, vmem_limit_bytes=56 * 1024 * 1024
        ),
    )(
        gather_pair(fwd_now), gather_pair(fwd_before), gather_pair(adj_now), gather_pair(adj_before),
        gather_pair(velocity), gather_pair(log_density),
        traces, rec_row[:, None], rec_row[None, :], rec_z[:, None],
        lists[1].astype(jnp.float32)[:, None], src_row[None, :], src_z[:, None], wavelet,
    )

    def split_pair(value):
        kept = lax.dynamic_slice_in_dim(value, side * tile_x, tile_x, axis=1)
        sent = lax.dynamic_slice_in_dim(value, (1 - side) * tile_x, tile_x, axis=1)
        got = lax.ppermute(sent, "xline", swap)
        return jnp.where(
            half == 0, jnp.concatenate([kept, got], axis=0), jnp.concatenate([got, kept], axis=0)
        )

    pieces = n_xline
    columns = lax.all_to_all(
        raw.reshape(n_i, n_x, pieces, depth // pieces).transpose(2, 0, 1, 3),
        "xline", split_axis=0, concat_axis=0, tiled=True,
    ).reshape(n_xline // 2, 2, n_i, n_x, depth // pieces)
    columns = jnp.where(core % 2 == 0, columns, columns[:, ::-1])
    positions = jnp.arange(full_x).astype(jnp.float32)
    weights = jnp.exp(-jnp.abs(positions[:, None] - positions[None, :]) / SMOOTH)
    weights = weights / jnp.sum(weights, axis=1, keepdims=True)
    gradient = jnp.einsum(
        "phixz,ypx->zhiy", columns, weights.reshape(full_x, n_xline // 2, n_x),
        precision=lax.Precision.HIGHEST,
    ).reshape(depth // pieces, tile_i, full_x)
    return gradient, split_pair(last), split_pair(previous)


def solution(mesh):
    return jax.shard_map(
        per_device,
        mesh=mesh,
        in_specs=(
            P(("shots", "inline"), "xline", None),
            P(("shots", "inline"), "xline", None),
            P(("shots", "inline"), "xline", None),
            P(("shots", "inline"), "xline", None),
            P("inline", "xline", None),
            P("inline", "xline", None),
            P("shots", ("xline", "inline")),
            P(("xline", "inline"), None),
            P(("xline", "inline"), None),
            P("shots"),
            P("shots", None),
        ),
        out_specs=(
            P(("shots", "xline"), "inline", None),
            P(("shots", "inline"), "xline", None),
            P(("shots", "inline"), "xline", None),
        ),
        check_vma=False,
    )
```

profile of v0, /device:TPU:0, one launch (start us, length us, event | category | flops | bytes accessed | tf_op | source)
XLA Modules:
  0.0 130.8 jit_solution(1831731496183048322)
XLA Ops:
  0.7 1.0 constant_dynamic-slice_fusion.13
  1.7 3.0 %collective-permute-start.1 = (f32[16,8,256]{2,1,0:T(8,128)S(1)}, f32[16,8,256]{2,1,0:T(8,128)S(1)}, u32[]{:S(2)}, u32[]{:S(2)}) collective-permute-start(f32[16,8,256]{2,1,0:T(8,128)S(1)} %get-tuple-element.37), channel_id=1, source_target_pairs={{0,2},{2,0},{4,6},{6,4},{8,10},{10,8},{12,14},{14,12},{1,3},{3,1},... | collective-permute-start | bytes 393224 | tf_op jit(solution)/shard_map/ppermute | solution.py:258
  4.9 2.1 %collective-permute-start.3 = (f32[16,8,256]{2,1,0:T(8,128)S(1)}, f32[16,8,256]{2,1,0:T(8,128)S(1)}, u32[]{:S(2)}, u32[]{:S(2)}) collective-permute-start(f32[16,8,256]{2,1,0:T(8,128)S(1)} %get-tuple-element.33), channel_id=1, source_target_pairs={{0,2},{2,0},{4,6},{6,4},{8,10},{10,8},{12,14},{14,12},{1,3},{3,1},... | collective-permute-start | bytes 393224 | tf_op jit(solution)/shard_map/ppermute | solution.py:258
  7.8 1.6 %collective-permute-start.7 = (s32[2,128]{1,0:T(2,128)S(1)}, s32[2,128]{1,0:T(2,128)S(1)}, u32[]{:S(2)}, u32[]{:S(2)}) collective-permute-start(s32[2,128]{1,0:T(2,128)S(1)} %pad_add_fusion), channel_id=1, source_target_pairs={{0,2},{2,0},{4,6},{6,4},{8,10},{10,8},{12,14},{14,12},{1,3},{3,1},... | collective-permute-start | bytes 3080 | tf_op jit(solution)/shard_map/ppermute | solution.py:263
  10.1 5.0 %all-to-all-start = ((f32[8,16,8]{2,0,1:T(8,128)}), f32[8,16,8]{2,0,1:T(8,128)S(1)}, u32[]{:S(2)}, u32[]{:S(2)}) async-start(f32[8,16,8]{2,0,1:T(8,128)} %copy.52), calls=%async_computation | async-start | bytes 131072 | tf_op jit(solution)/shard_map/all_to_all | solution.py:260
  15.2 0.9 copy-done.5
  19.0 3.0 %all-to-all-done = f32[8,16,8]{2,0,1:T(8,128)S(1)} async-done(((f32[8,16,8]{2,0,1:T(8,128)}), f32[8,16,8]{2,0,1:T(8,128)S(1)}, u32[]{:S(2)}, u32[]{:S(2)}) %all-to-all-start) | async-done | bytes 4128 | tf_op jit(solution)/shard_map/all_to_all | solution.py:260
  22.3 0.9 add_select_fusion
  23.3 0.8 copy.60.rec_live
  24.1 1.7 %collective-permute-done.6 = f32[8,128]{1,0:T(8,128)S(1)} collective-permute-done((f32[8,128]{1,0:T(8,128)S(1)}, f32[8,128]{1,0:T(8,128)S(1)}, u32[]{:S(2)}, u32[]{:S(2)}) %collective-permute-start.6) | collective-permute-done | bytes 4128 | tf_op jit(solution)/shard_map/ppermute | solution.py:264
  26.9 1.9 %collective-permute-start = (f32[16,8,256]{2,1,0:T(8,128)S(1)}, f32[16,8,256]{2,1,0:T(8,128)S(1)}, u32[]{:S(2)}, u32[]{:S(2)}) collective-permute-start(f32[16,8,256]{2,1,0:T(8,128)S(1)} %get-tuple-element.39), channel_id=1, source_target_pairs={{0,2},{2,0},{4,6},{6,4},{8,10},{10,8},{12,14},{14,12},{1,3},{3,1},... | collective-permute-start | bytes 393224 | tf_op jit(solution)/shard_map/ppermute | solution.py:258
  31.0 0.7 maximum_select_fusion.4.velocity
  31.7 0.7 maximum_select_fusion.5.density
  33.5 76.8 %shard_map.130 = (f32[16,16,256]{2,1,0:T(8,128)}, f32[16,16,256]{2,1,0:T(8,128)}, f32[16,16,256]{2,1,0:T(8,128)}) custom-call(f32[16,16,256]{2,1,0:T(8,128)} %maximum_select_fusion.fwd_now, f32[16,16,256]{2,1,0:T(8,128)} %maximum_select_fusion.1.fwd_before, f32[16,16,256]{2,1,0:T(8,128)} %maximum_select_fusion.2.adj_now, ...), custom_call_target="tpu_custom_call" | custom-call | tf_op jit(solution)/shard_map/pallas_call | solution.py:281
  110.2 1.0 constant_dynamic-slice_fusion.1
  112.1 1.2 reshape.298
  113.3 4.1 %all-to-all-start.1 = ((f32[8,1,8192]{2,1,0:T(1,128)}), f32[8,1,8192]{2,1,0:T(1,128)S(1)}, u32[]{:S(2)}, u32[]{:S(2)}) async-start(f32[8,1,8192]{2,1,0:T(1,128)} %reshape.298), calls=%async_computation.1 | async-start | bytes 524288 | tf_op jit(solution)/shard_map/all_to_all | solution.py:323
  117.4 2.1 %collective-permute-start.8 = (f32[16,8,256]{2,1,0:T(8,128)S(1)}, f32[16,8,256]{2,1,0:T(8,128)S(1)}, u32[]{:S(2)}, u32[]{:S(2)}) collective-permute-start(f32[16,8,256]{2,1,0:T(8,128)S(1)} %get-tuple-element.27), channel_id=1, source_target_pairs={{0,2},{2,0},{4,6},{6,4},{8,10},{10,8},{12,14},{14,12},{1,3},{3,1},... | collective-permute-start | bytes 393224 | tf_op jit(solution)/shard_map/ppermute | solution.py:317
  119.5 0.7 maximum_select_fusion.7
  120.2 3.7 %collective-permute-done.8 = f32[16,8,256]{2,1,0:T(8,128)S(1)} collective-permute-done((f32[16,8,256]{2,1,0:T(8,128)S(1)}, f32[16,8,256]{2,1,0:T(8,128)S(1)}, u32[]{:S(2)}, u32[]{:S(2)}) %collective-permute-start.8) | collective-permute-done | bytes 131104 | tf_op jit(solution)/shard_map/ppermute | solution.py:317
  124.7 0.9 all-to-all-done.1
  126.1 1.3 reduce
  127.8 1.8 %fusion.8 = f32[64,2,16,32,1]{0,3,2,1,4:T(8,128)S(1)} fusion(f32[4,2,16,16,32]{4,3,2,1,0:T(8,128)S(1)} %reverse_select_fusion, f32[64]{0:T(128)S(1)} %exponential_reduce_fusion, f32[4,16]{1,0:T(4,128)S(1)} %add_convert_fusion, f32[64]{0:T(128)S(1)} %iota_convert_fusion), kind=kOutput, calls=%fused_computation.32 | convolution fusion | flops 50352128 | bytes 525056 | tf_op jit(solution)/shard_map/phixz,ypx->zhiy/dot_general | solution.py:331
  129.7 1.1 copy.64
  (69 shorter events, 11.8 us)
Async XLA Ops:
  0.7 4.1 %copy-start.1 = (f32[32,8,256]{2,1,0:T(8,128)S(1)}, f32[32,8,256]{2,1,0:T(8,128)}, u32[]{:S(2)}) copy-start(f32[32,8,256]{2,1,0:T(8,128)} %param.13) | copy-start | bytes 786436
  1.7 3.2 %copy-start.2 = (f32[32,8,256]{2,1,0:T(8,128)S(1)}, f32[32,8,256]{2,1,0:T(8,128)}, u32[]{:S(2)}) copy-start(f32[32,8,256]{2,1,0:T(8,128)} %param.14) | copy-start | bytes 786436
  1.7 25.2 %collective-permute-start.1 = (f32[16,8,256]{2,1,0:T(8,128)S(1)}, f32[16,8,256]{2,1,0:T(8,128)S(1)}, u32[]{:S(2)}, u32[]{:S(2)}) collective-permute-start(f32[16,8,256]{2,1,0:T(8,128)S(1)} %get-tuple-element.37), channel_id=1, source_target_pairs={{0,2},{2,0},{4,6},{6,4},{8,10},{10,8},{12,14},{14,12},{1,3},{3,1},... | collective-permute-start | bytes 393224 | tf_op jit(solution)/shard_map/ppermute | solution.py:258
  4.8 2.2 %copy-start.3 = (f32[32,8,256]{2,1,0:T(8,128)S(1)}, f32[32,8,256]{2,1,0:T(8,128)}, u32[]{:S(2)}) copy-start(f32[32,8,256]{2,1,0:T(8,128)} %param.15) | copy-start | bytes 786436
  4.8 24.7 %collective-permute-start.2 = (f32[16,8,256]{2,1,0:T(8,128)S(1)}, f32[16,8,256]{2,1,0:T(8,128)S(1)}, u32[]{:S(2)}, u32[]{:S(2)}) collective-permute-start(f32[16,8,256]{2,1,0:T(8,128)S(1)} %get-tuple-element.35), channel_id=1, source_target_pairs={{0,2},{2,0},{4,6},{6,4},{8,10},{10,8},{12,14},{14,12},{1,3},{3,1},... | collective-permute-start | bytes 393224 | tf_op jit(solution)/shard_map/ppermute | solution.py:258
  4.9 25.3 %collective-permute-start.3 = (f32[16,8,256]{2,1,0:T(8,128)S(1)}, f32[16,8,256]{2,1,0:T(8,128)S(1)}, u32[]{:S(2)}, u32[]{:S(2)}) collective-permute-start(f32[16,8,256]{2,1,0:T(8,128)S(1)} %get-tuple-element.33), channel_id=1, source_target_pairs={{0,2},{2,0},{4,6},{6,4},{8,10},{10,8},{12,14},{14,12},{1,3},{3,1},... | collective-permute-start | bytes 393224 | tf_op jit(solution)/shard_map/ppermute | solution.py:258
  7.0 0.7 copy-start.9
  7.0 0.8 copy-start.8
  7.0 2.4 %copy-start.7 = (f32[8,128]{1,0:T(8,128)S(1)}, f32[8,128]{1,0:T(8,128)}, u32[]{:S(2)}) copy-start(f32[8,128]{1,0:T(8,128)} %param.17) | copy-start | bytes 12292
  7.0 8.1 %copy-start.4 = (f32[32,8,256]{2,1,0:T(8,128)S(1)}, f32[32,8,256]{2,1,0:T(8,128)}, u32[]{:S(2)}) copy-start(f32[32,8,256]{2,1,0:T(8,128)} %param.16) | copy-start | bytes 786436
  7.0 23.9 %collective-permute-start.4 = (f32[16,8,256]{2,1,0:T(8,128)S(1)}, f32[16,8,256]{2,1,0:T(8,128)S(1)}, u32[]{:S(2)}, u32[]{:S(2)}) collective-permute-start(f32[16,8,256]{2,1,0:T(8,128)S(1)} %get-tuple-element.31), channel_id=1, source_target_pairs={{0,2},{2,0},{4,6},{6,4},{8,10},{10,8},{12,14},{14,12},{1,3},{3,1},... | collective-permute-start | bytes 393224 | tf_op jit(solution)/shard_map/ppermute | solution.py:258
  7.8 10.4 %collective-permute-start.7 = (s32[2,128]{1,0:T(2,128)S(1)}, s32[2,128]{1,0:T(2,128)S(1)}, u32[]{:S(2)}, u32[]{:S(2)}) collective-permute-start(s32[2,128]{1,0:T(2,128)S(1)} %pad_add_fusion), channel_id=1, source_target_pairs={{0,2},{2,0},{4,6},{6,4},{8,10},{10,8},{12,14},{14,12},{1,3},{3,1},... | collective-permute-start | bytes 3080 | tf_op jit(solution)/shard_map/ppermute | solution.py:263
  10.1 11.9 %all-to-all-start = ((f32[8,16,8]{2,0,1:T(8,128)}), f32[8,16,8]{2,0,1:T(8,128)S(1)}, u32[]{:S(2)}, u32[]{:S(2)}) async-start(f32[8,16,8]{2,0,1:T(8,128)} %copy.52), calls=%async_computation | async-start | bytes 131072 | tf_op jit(solution)/shard_map/all_to_all | solution.py:260
  15.1 1.0 copy-start.5
  16.1 0.7 copy-start.10
  22.1 3.7 %collective-permute-start.6 = (f32[8,128]{1,0:T(8,128)S(1)}, f32[8,128]{1,0:T(8,128)S(1)}, u32[]{:S(2)}, u32[]{:S(2)}) collective-permute-start(f32[8,128]{1,0:T(8,128)S(1)} %all_to_all.13), channel_id=1, source_target_pairs={{0,2},{2,0},{4,6},{6,4},{8,10},{10,8},{12,14},{14,12},{1,3},{3,1},... | collective-permute-start | bytes 12296 | tf_op jit(solution)/shard_map/ppermute | solution.py:264
  25.8 5.9 %collective-permute-start.5 = (f32[16,8,256]{2,1,0:T(8,128)S(1)}, f32[16,8,256]{2,1,0:T(8,128)S(1)}, u32[]{:S(2)}, u32[]{:S(2)}) collective-permute-start(f32[16,8,256]{2,1,0:T(8,128)S(1)} %get-tuple-element.29), channel_id=1, source_target_pairs={{0,2},{2,0},{4,6},{6,4},{8,10},{10,8},{12,14},{14,12},{1,3},{3,1},... | collective-permute-start | bytes 393224 | tf_op jit(solution)/shard_map/ppermute | solution.py:258
  26.9 5.8 %collective-permute-start = (f32[16,8,256]{2,1,0:T(8,128)S(1)}, f32[16,8,256]{2,1,0:T(8,128)S(1)}, u32[]{:S(2)}, u32[]{:S(2)}) collective-permute-start(f32[16,8,256]{2,1,0:T(8,128)S(1)} %get-tuple-element.39), channel_id=1, source_target_pairs={{0,2},{2,0},{4,6},{6,4},{8,10},{10,8},{12,14},{14,12},{1,3},{3,1},... | collective-permute-start | bytes 393224 | tf_op jit(solution)/shard_map/ppermute | solution.py:258
  110.2 1.4 %copy-start = (f32[16,16,256]{2,1,0:T(8,128)S(1)}, f32[16,16,256]{2,1,0:T(8,128)}, u32[]{:S(2)}) copy-start(f32[16,16,256]{2,1,0:T(8,128)} %get-tuple-element.6) | copy-start | bytes 786436
  111.3 8.2 %collective-permute-start.9 = (f32[16,8,256]{2,1,0:T(8,128)S(1)}, f32[16,8,256]{2,1,0:T(8,128)S(1)}, u32[]{:S(2)}, u32[]{:S(2)}) collective-permute-start(f32[16,8,256]{2,1,0:T(8,128)S(1)} %get-tuple-element.25), channel_id=1, source_target_pairs={{0,2},{2,0},{4,6},{6,4},{8,10},{10,8},{12,14},{14,12},{1,3},{3,1},... | collective-permute-start | bytes 393224 | tf_op jit(solution)/shard_map/ppermute | solution.py:317
  113.3 4.1 %copy-start.6 = (f32[16,16,256]{2,1,0:T(8,128)S(1)}, f32[16,16,256]{2,1,0:T(8,128)}, u32[]{:S(2)}) copy-start(f32[16,16,256]{2,1,0:T(8,128)} %get-tuple-element.7) | copy-start | bytes 786436
  113.3 12.3 %all-to-all-start.1 = ((f32[8,1,8192]{2,1,0:T(1,128)}), f32[8,1,8192]{2,1,0:T(1,128)S(1)}, u32[]{:S(2)}, u32[]{:S(2)}) async-start(f32[8,1,8192]{2,1,0:T(1,128)} %reshape.298), calls=%async_computation.1 | async-start | bytes 524288 | tf_op jit(solution)/shard_map/all_to_all | solution.py:323
  117.4 6.5 %collective-permute-start.8 = (f32[16,8,256]{2,1,0:T(8,128)S(1)}, f32[16,8,256]{2,1,0:T(8,128)S(1)}, u32[]{:S(2)}, u32[]{:S(2)}) collective-permute-start(f32[16,8,256]{2,1,0:T(8,128)S(1)} %get-tuple-element.27), channel_id=1, source_target_pairs={{0,2},{2,0},{4,6},{6,4},{8,10},{10,8},{12,14},{14,12},{1,3},{3,1},... | collective-permute-start | bytes 393224 | tf_op jit(solution)/shard_map/ppermute | solution.py:317
where the time goes:
time: 131 us
  Pallas kernels  76.8 us (59%)
  starting transfers between devices  20.6 us (16%)
  local copies, waits for them, and re-layouts  10.7 us (8%)
  other arithmetic  10.3 us (8%)
  waiting for transfers between devices  9.69 us (7%)
  matrix products  1.84 us (1%)
    pallas_call x1, Pallas kernels, per_device(): pl.pallas_call(kernel, out_shape=[jax.ShapeDtypeStruct(block, jnp.float32...  76.8 us
    ppermute x6, starting transfers between devices, gather_pair(): return pair_up(kept, lax.ppermute(sent, 'xline', swap), 1)  7.33 us
    all_to_all x1, starting transfers between devices, per_device(): lax.all_to_all(observed, ('xline', 'inline'), split_axis=1, concat_axis=1...  4.98 us
    unnamed x25, local copies, waits for them, and re-layouts  4.68 us
    select_n x7, other arithmetic, pair_up(): jnp.where(side == 0, jnp.concatenate([mine, theirs], axis=axis), jnp.conc...  4.36 us
    all_to_all x1, starting transfers between devices, per_device(): lax.all_to_all(raw.reshape(n_i, n_x, pieces, depth // pieces).transpose(2...  4.07 us
    ppermute x2, waiting for transfers between devices, split_pair(): got = lax.ppermute(sent, 'xline', swap)  3.73 us
    all_to_all x1, waiting for transfers between devices, per_device(): lax.all_to_all(observed, ('xline', 'inline'), split_axis=1, concat_axis=1...  2.99 us
  transfers between devices with their start and end apart: 12, of which 5 were waited for; matrix products, arithmetic and copies ran while one was open for 10% of the time, Pallas kernels for 0%

commit v1 on v0

--- a/solution.py
+++ b/solution.py
@@ -57,11 +57,17 @@
     )
     inner_x = pl.ds(8, n_x)
 
-    def copy_of(idx, way):
+    middle = n_i // 2
+
+    def copy_of(idx, way, part):
+        part_rows = pl.ds(part * middle, middle)
+        sem = way
         if way == LEFT:
-            src, dst = x_out.at[idx, 0], x_in.at[idx, 1]
+            src, dst = x_out.at[idx, 0, part_rows], x_in.at[idx, 1, part_rows]
+            sem = way + 4 * part
         elif way == RIGHT:
-            src, dst = x_out.at[idx, 1], x_in.at[idx, 0]
+            src, dst = x_out.at[idx, 1, part_rows], x_in.at[idx, 0, part_rows]
+            sem = way + 4 * part
         elif way == UP:
             src = field.at[idx, pl.ds(4, 4), inner_x, :]
             dst = field.at[idx, pl.ds(n_i + 4, 4), inner_x, :]
@@ -70,26 +76,30 @@
             dst = field.at[idx, pl.ds(0, 4), inner_x, :]
         return pltpu.make_async_remote_copy(
             src_ref=src, dst_ref=dst,
-            send_sem=send_sem.at[idx, way], recv_sem=recv_sem.at[idx, way],
+            send_sem=send_sem.at[idx, sem], recv_sem=recv_sem.at[idx, sem],
             device_id=target[way], device_id_type=MESH,
         )
 
-    def send(idx):
-        x_out[idx, 0] = field[idx, pl.ds(4, n_i), pl.ds(8, 4), :]
-        x_out[idx, 1] = field[idx, pl.ds(4, n_i), pl.ds(4 + n_x, 4), :]
-        for way in range(4):
+    def send(idx, part):
+        part_rows = pl.ds(part * middle, middle)
+        field_rows = pl.ds(4 + part * middle, middle)
+        x_out[idx, 0, part_rows] = field[idx, field_rows, pl.ds(8, 4), :]
+        x_out[idx, 1, part_rows] = field[idx, field_rows, pl.ds(4 + n_x, 4), :]
+        for way in (LEFT, RIGHT, UP + part):
             @pl.when(has[way])
             def _():
-                copy_of(idx, way).start()
-
-    def finish(idx):
-        for way in range(4):
+                copy_of(idx, way, part).start()
+
+    def finish(idx, part):
+        for way in (LEFT, RIGHT, UP + part):
             @pl.when(has[way])
             def _():
-                copy_of(idx, way).wait_send()
-                copy_of(idx, way ^ 1).wait_recv()
-        field[idx, pl.ds(4, n_i), pl.ds(4, 4), :] = x_in[idx, 0]
-        field[idx, pl.ds(4, n_i), pl.ds(8 + n_x, 4), :] = x_in[idx, 1]
+                copy_of(idx, way, part).wait_send()
+                copy_of(idx, way ^ 1, part).wait_recv()
+        part_rows = pl.ds(part * middle, middle)
+        field_rows = pl.ds(4 + part * middle, middle)
+        field[idx, field_rows, pl.ds(4, 4), :] = x_in[idx, 0, part_rows]
+        field[idx, field_rows, pl.ds(8 + n_x, 4), :] = x_in[idx, 1, part_rows]
 
     for idx in range(5):
         field[idx, pl.ds(0, 4)] = jnp.zeros((4,) + field.shape[2:], jnp.float32)
@@ -106,10 +116,13 @@
     inner_i = pl.ds(4, n_i)
     field[DENSITY, inner_i, inner_x, :] = density[...]
     field[0, inner_i, inner_x, :] = fwd_now[...]
-    send(DENSITY)
-    send(0)
+    send(DENSITY, 0)
+    send(DENSITY, 1)
+    send(0, 0)
+    send(0, 1)
     field[2, inner_i, inner_x, :] = adj_now[...]
-    send(2)
+    send(2, 0)
+    send(2, 1)
     field[1, inner_i, inner_x, :] = fwd_before[...]
     field[3, inner_i, inner_x, :] = adj_before[...]
 
@@ -167,7 +180,8 @@
         base[...] = partial.reshape(n_i, n_x, depth)
 
     slopes[2] = along_depth(DENSITY)[1].reshape(n_i, n_x, depth)
-    finish(DENSITY)
+    finish(DENSITY, 0)
+    finish(DENSITY, 1)
 
     @pl.loop(0, n_i)
     def _(i):
@@ -181,20 +195,22 @@
         other = 1 - now
         high, low = split_bf16(src_rows * wavelet[pl.ds(t, 1), :])
         prepare(now, dot(high, src_cols) + dot(low, src_cols))
-        finish(now)
-
-        @pl.loop(0, n_i)
-        def _(i):
-            lap, slope_i, slope_x = across(now, i)
-            change = base[i] + speed_sq[i] * (lap - slopes[0, i] * slope_i - slopes[1, i] * slope_x)
-            accel[t, i] = change
-            field[other, i + 4, inner_x, :] = (
-                2.0 * field[now, i + 4, inner_x, :] - field[other, i + 4, inner_x, :] + change
-            )
-
-        @pl.when(t < steps - 1)
-        def _():
-            send(other)
+
+        for part in range(2):
+            finish(now, part)
+
+            @pl.loop(part * middle, (part + 1) * middle)
+            def _(i):
+                lap, slope_i, slope_x = across(now, i)
+                change = base[i] + speed_sq[i] * (lap - slopes[0, i] * slope_i - slopes[1, i] * slope_x)
+                accel[t, i] = change
+                field[other, i + 4, inner_x, :] = (
+                    2.0 * field[now, i + 4, inner_x, :] - field[other, i + 4, inner_x, :] + change
+                )
+
+            @pl.when(t < steps - 1)
+            def _():
+                send(other, part)
 
         high, low = split_bf16(flat(other))
         picked = dot(row_map_t[...], high) + dot(row_map_t[...], low)
@@ -210,19 +226,21 @@
         t = steps - 1 - j
         high, low = split_bf16(residual_ref[t] * z_map[...])
         prepare(now, dot(row_map[...], high) + dot(row_map[...], low))
-        finish(now)
-
-        @pl.loop(0, n_i)
-        def _(i):
-            lap, slope_i, slope_x = across(now, i)
-            change = base[i] + speed_sq[i] * (lap - slopes[0, i] * slope_i - slopes[1, i] * slope_x)
-            fresh = 2.0 * field[now, i + 4, inner_x, :] - field[other, i + 4, inner_x, :] + change
-            field[other, i + 4, inner_x, :] = fresh
-            image[i] += fresh * accel[t, i]
-
-        @pl.when(j < steps - 1)
-        def _():
-            send(other)
+
+        for part in range(2):
+            finish(now, part)
+
+            @pl.loop(part * middle, (part + 1) * middle)
+            def _(i):
+                lap, slope_i, slope_x = across(now, i)
+                change = base[i] + speed_sq[i] * (lap - slopes[0, i] * slope_i - slopes[1, i] * slope_x)
+                fresh = 2.0 * field[now, i + 4, inner_x, :] - field[other, i + 4, inner_x, :] + change
+                field[other, i + 4, inner_x, :] = fresh
+                image[i] += fresh * accel[t, i]
+
+            @pl.when(j < steps - 1)
+            def _():
+                send(other, part)
 
     raw_out[...] = image[...] * (2.0 / steps) / velocity[...]
     last_out[...] = field[2 + steps % 2, inner_i, inner_x, :]
@@ -298,8 +316,8 @@
             pltpu.VMEM((depth, 2 * depth), jnp.bfloat16),
             pltpu.VMEM((depth, 2 * depth), jnp.bfloat16),
             pltpu.VMEM((steps, slots, 1), jnp.float32),
-            pltpu.SemaphoreType.DMA((5, 4)),
-            pltpu.SemaphoreType.DMA((5, 4)),
+            pltpu.SemaphoreType.DMA((5, 6)),
+            pltpu.SemaphoreType.DMA((5, 6)),
         ],
         compiler_params=pltpu.CompilerParams(
             collective_id=0, has_side_effects=True, vmem_limit_bytes=56 * 1024 * 1024

time: 131 us -> 120 us (0.916)
  Pallas kernels: 76.8 us -> 65.1 us
    pallas_call x1, Pallas kernels: 76.8 us -> 65.1 us  [per_device(): pl.pallas_call(kernel, out_shape=[jax.ShapeDtypeStruct(block, jnp.float32...]
  transfers between devices with their start and end apart: 12 -> 12, of which waited for: 5 -> 5; matrix products, arithmetic and copies ran while one was open for 10% -> 11% of each run, Pallas kernels for 0% -> 0%
where the time goes in v1:
time: 120 us; the launch traced here: 119 us
  Pallas kernels  65.1 us (54%)
  starting transfers between devices  20.7 us (17%)
  local copies, waits for them, and re-layouts  10.7 us (9%)
  other arithmetic  10.3 us (9%)
  waiting for transfers between devices  9.72 us (8%)
  matrix products  1.84 us (2%)
    pallas_call x1, Pallas kernels, per_device(): pl.pallas_call(kernel, out_shape=[jax.ShapeDtypeStruct(block, jnp.float32...  65.1 us
    ppermute x6, starting transfers between devices, gather_pair(): return pair_up(kept, lax.ppermute(sent, 'xline', swap), 1)  7.33 us
    all_to_all x1, starting transfers between devices, per_device(): lax.all_to_all(observed, ('xline', 'inline'), split_axis=1, concat_axis=1...  4.98 us
    unnamed x25, local copies, waits for them, and re-layouts  4.68 us
    select_n x7, other arithmetic, pair_up(): jnp.where(side == 0, jnp.concatenate([mine, theirs], axis=axis), jnp.conc...  4.36 us
    all_to_all x1, starting transfers between devices, per_device(): lax.all_to_all(raw.reshape(n_i, n_x, pieces, depth // pieces).transpose(2...  3.59 us
    ppermute x2, waiting for transfers between devices, split_pair(): got = lax.ppermute(sent, 'xline', swap)  3.31 us
    ppermute x2, starting transfers between devices, split_pair(): got = lax.ppermute(sent, 'xline', swap)  3 us
  transfers between devices with their start and end apart: 12, of which 5 were waited for; matrix products, arithmetic and copies ran while one was open for 11% of the time, Pallas kernels for 0%

profile of v1, /device:TPU:0, one launch (start us, length us, event | category | flops | bytes accessed | tf_op | source)
XLA Modules:
  0.0 119.2 jit_solution(9244143282461702398)
XLA Ops:
  0.7 1.0 constant_dynamic-slice_fusion.13
  1.7 3.0 %collective-permute-start.1 = (f32[16,8,256]{2,1,0:T(8,128)S(1)}, f32[16,8,256]{2,1,0:T(8,128)S(1)}, u32[]{:S(2)}, u32[]{:S(2)}) collective-permute-start(f32[16,8,256]{2,1,0:T(8,128)S(1)} %get-tuple-element.37), channel_id=1, source_target_pairs={{0,2},{2,0},{4,6},{6,4},{8,10},{10,8},{12,14},{14,12},{1,3},{3,1},... | collective-permute-start | bytes 393224 | tf_op jit(solution)/shard_map/ppermute | solution.py:276
  4.9 2.1 %collective-permute-start.3 = (f32[16,8,256]{2,1,0:T(8,128)S(1)}, f32[16,8,256]{2,1,0:T(8,128)S(1)}, u32[]{:S(2)}, u32[]{:S(2)}) collective-permute-start(f32[16,8,256]{2,1,0:T(8,128)S(1)} %get-tuple-element.33), channel_id=1, source_target_pairs={{0,2},{2,0},{4,6},{6,4},{8,10},{10,8},{12,14},{14,12},{1,3},{3,1},... | collective-permute-start | bytes 393224 | tf_op jit(solution)/shard_map/ppermute | solution.py:276
  7.8 1.6 %collective-permute-start.7 = (s32[2,128]{1,0:T(2,128)S(1)}, s32[2,128]{1,0:T(2,128)S(1)}, u32[]{:S(2)}, u32[]{:S(2)}) collective-permute-start(s32[2,128]{1,0:T(2,128)S(1)} %pad_add_fusion), channel_id=1, source_target_pairs={{0,2},{2,0},{4,6},{6,4},{8,10},{10,8},{12,14},{14,12},{1,3},{3,1},... | collective-permute-start | bytes 3080 | tf_op jit(solution)/shard_map/ppermute | solution.py:281
  10.1 5.0 %all-to-all-start = ((f32[8,16,8]{2,0,1:T(8,128)}), f32[8,16,8]{2,0,1:T(8,128)S(1)}, u32[]{:S(2)}, u32[]{:S(2)}) async-start(f32[8,16,8]{2,0,1:T(8,128)} %copy.52), calls=%async_computation | async-start | bytes 131072 | tf_op jit(solution)/shard_map/all_to_all | solution.py:278
  15.2 0.9 copy-done.5
  19.0 3.0 %all-to-all-done = f32[8,16,8]{2,0,1:T(8,128)S(1)} async-done(((f32[8,16,8]{2,0,1:T(8,128)}), f32[8,16,8]{2,0,1:T(8,128)S(1)}, u32[]{:S(2)}, u32[]{:S(2)}) %all-to-all-start) | async-done | bytes 4128 | tf_op jit(solution)/shard_map/all_to_all | solution.py:278
  22.3 0.9 add_select_fusion
  23.3 0.8 copy.60.rec_live
  24.1 1.7 %collective-permute-done.6 = f32[8,128]{1,0:T(8,128)S(1)} collective-permute-done((f32[8,128]{1,0:T(8,128)S(1)}, f32[8,128]{1,0:T(8,128)S(1)}, u32[]{:S(2)}, u32[]{:S(2)}) %collective-permute-start.6) | collective-permute-done | bytes 4128 | tf_op jit(solution)/shard_map/ppermute | solution.py:282
  26.9 1.9 %collective-permute-start = (f32[16,8,256]{2,1,0:T(8,128)S(1)}, f32[16,8,256]{2,1,0:T(8,128)S(1)}, u32[]{:S(2)}, u32[]{:S(2)}) collective-permute-start(f32[16,8,256]{2,1,0:T(8,128)S(1)} %get-tuple-element.39), channel_id=1, source_target_pairs={{0,2},{2,0},{4,6},{6,4},{8,10},{10,8},{12,14},{14,12},{1,3},{3,1},... | collective-permute-start | bytes 393224 | tf_op jit(solution)/shard_map/ppermute | solution.py:276
  31.0 0.7 maximum_select_fusion.4.velocity
  31.7 0.7 maximum_select_fusion.5.density
  33.5 65.1 %shard_map.130 = (f32[16,16,256]{2,1,0:T(8,128)}, f32[16,16,256]{2,1,0:T(8,128)}, f32[16,16,256]{2,1,0:T(8,128)}) custom-call(f32[16,16,256]{2,1,0:T(8,128)} %maximum_select_fusion.fwd_now, f32[16,16,256]{2,1,0:T(8,128)} %maximum_select_fusion.1.fwd_before, f32[16,16,256]{2,1,0:T(8,128)} %maximum_select_fusion.2.adj_now, ...), custom_call_target="tpu_custom_call" | custom-call | tf_op jit(solution)/shard_map/pallas_call | solution.py:299
  98.6 1.0 constant_dynamic-slice_fusion.1
  99.7 0.9 collective-permute-start.9
  101.1 1.2 reshape.298
  102.2 3.6 %all-to-all-start.1 = ((f32[8,1,8192]{2,1,0:T(1,128)}), f32[8,1,8192]{2,1,0:T(1,128)S(1)}, u32[]{:S(2)}, u32[]{:S(2)}) async-start(f32[8,1,8192]{2,1,0:T(1,128)} %reshape.298), calls=%async_computation.1 | async-start | bytes 524288 | tf_op jit(solution)/shard_map/all_to_all | solution.py:341
  105.9 2.1 %collective-permute-start.8 = (f32[16,8,256]{2,1,0:T(8,128)S(1)}, f32[16,8,256]{2,1,0:T(8,128)S(1)}, u32[]{:S(2)}, u32[]{:S(2)}) collective-permute-start(f32[16,8,256]{2,1,0:T(8,128)S(1)} %get-tuple-element.27), channel_id=1, source_target_pairs={{0,2},{2,0},{4,6},{6,4},{8,10},{10,8},{12,14},{14,12},{1,3},{3,1},... | collective-permute-start | bytes 393224 | tf_op jit(solution)/shard_map/ppermute | solution.py:335
  108.7 3.3 %collective-permute-done.8 = f32[16,8,256]{2,1,0:T(8,128)S(1)} collective-permute-done((f32[16,8,256]{2,1,0:T(8,128)S(1)}, f32[16,8,256]{2,1,0:T(8,128)S(1)}, u32[]{:S(2)}, u32[]{:S(2)}) %collective-permute-start.8) | collective-permute-done | bytes 131104 | tf_op jit(solution)/shard_map/ppermute | solution.py:335
  112.7 1.4 %all-to-all-done.1 = f32[8,1,8192]{2,1,0:T(1,128)S(1)} async-done(((f32[8,1,8192]{2,1,0:T(1,128)}), f32[8,1,8192]{2,1,0:T(1,128)S(1)}, u32[]{:S(2)}, u32[]{:S(2)}) %all-to-all-start.1) | async-done | bytes 262176 | tf_op jit(solution)/shard_map/all_to_all | solution.py:341
  114.6 1.3 %reduce = f32[8,8192]{1,0:T(8,128)S(1)} reduce(f32[8,1,8192]{2,1,0:T(1,128)S(1)} %all-to-all-done.1, f32[]{:T(128)} %broadcast.347), dimensions={1}, to_apply=%all_to_all.14.reduce_sub_computation | reduce | bytes 524292 | tf_op jit(solution)/shard_map/all_to_all | solution.py:341
  116.3 1.8 %fusion.8 = f32[64,2,16,32,1]{0,3,2,1,4:T(8,128)S(1)} fusion(f32[4,2,16,16,32]{4,3,2,1,0:T(8,128)S(1)} %reverse_select_fusion, f32[64]{0:T(128)S(1)} %exponential_reduce_fusion, f32[4,16]{1,0:T(4,128)S(1)} %add_convert_fusion, f32[64]{0:T(128)S(1)} %iota_convert_fusion), kind=kOutput, calls=%fused_computation.32 | convolution fusion | flops 50352128 | bytes 525056 | tf_op jit(solution)/shard_map/phixz,ypx->zhiy/dot_general | solution.py:349
  118.1 1.1 copy.64
  (69 shorter events, 12.1 us)
Async XLA Ops:
  0.7 4.1 %copy-start.1 = (f32[32,8,256]{2,1,0:T(8,128)S(1)}, f32[32,8,256]{2,1,0:T(8,128)}, u32[]{:S(2)}) copy-start(f32[32,8,256]{2,1,0:T(8,128)} %param.13) | copy-start | bytes 786436
  1.7 3.2 %copy-start.2 = (f32[32,8,256]{2,1,0:T(8,128)S(1)}, f32[32,8,256]{2,1,0:T(8,128)}, u32[]{:S(2)}) copy-start(f32[32,8,256]{2,1,0:T(8,128)} %param.14) | copy-start | bytes 786436
  1.7 25.2 %collective-permute-start.1 = (f32[16,8,256]{2,1,0:T(8,128)S(1)}, f32[16,8,256]{2,1,0:T(8,128)S(1)}, u32[]{:S(2)}, u32[]{:S(2)}) collective-permute-start(f32[16,8,256]{2,1,0:T(8,128)S(1)} %get-tuple-element.37), channel_id=1, source_target_pairs={{0,2},{2,0},{4,6},{6,4},{8,10},{10,8},{12,14},{14,12},{1,3},{3,1},... | collective-permute-start | bytes 393224 | tf_op jit(solution)/shard_map/ppermute | solution.py:276
  4.8 2.2 %copy-start.3 = (f32[32,8,256]{2,1,0:T(8,128)S(1)}, f32[32,8,256]{2,1,0:T(8,128)}, u32[]{:S(2)}) copy-start(f32[32,8,256]{2,1,0:T(8,128)} %param.15) | copy-start | bytes 786436
  4.8 24.7 %collective-permute-start.2 = (f32[16,8,256]{2,1,0:T(8,128)S(1)}, f32[16,8,256]{2,1,0:T(8,128)S(1)}, u32[]{:S(2)}, u32[]{:S(2)}) collective-permute-start(f32[16,8,256]{2,1,0:T(8,128)S(1)} %get-tuple-element.35), channel_id=1, source_target_pairs={{0,2},{2,0},{4,6},{6,4},{8,10},{10,8},{12,14},{14,12},{1,3},{3,1},... | collective-permute-start | bytes 393224 | tf_op jit(solution)/shard_map/ppermute | solution.py:276
  4.9 25.3 %collective-permute-start.3 = (f32[16,8,256]{2,1,0:T(8,128)S(1)}, f32[16,8,256]{2,1,0:T(8,128)S(1)}, u32[]{:S(2)}, u32[]{:S(2)}) collective-permute-start(f32[16,8,256]{2,1,0:T(8,128)S(1)} %get-tuple-element.33), channel_id=1, source_target_pairs={{0,2},{2,0},{4,6},{6,4},{8,10},{10,8},{12,14},{14,12},{1,3},{3,1},... | collective-permute-start | bytes 393224 | tf_op jit(solution)/shard_map/ppermute | solution.py:276
  7.0 0.7 copy-start.9
  7.0 0.8 copy-start.8
  7.0 2.4 %copy-start.7 = (f32[8,128]{1,0:T(8,128)S(1)}, f32[8,128]{1,0:T(8,128)}, u32[]{:S(2)}) copy-start(f32[8,128]{1,0:T(8,128)} %param.17) | copy-start | bytes 12292
  7.0 8.1 %copy-start.4 = (f32[32,8,256]{2,1,0:T(8,128)S(1)}, f32[32,8,256]{2,1,0:T(8,128)}, u32[]{:S(2)}) copy-start(f32[32,8,256]{2,1,0:T(8,128)} %param.16) | copy-start | bytes 786436
  7.0 23.9 %collective-permute-start.4 = (f32[16,8,256]{2,1,0:T(8,128)S(1)}, f32[16,8,256]{2,1,0:T(8,128)S(1)}, u32[]{:S(2)}, u32[]{:S(2)}) collective-permute-start(f32[16,8,256]{2,1,0:T(8,128)S(1)} %get-tuple-element.31), channel_id=1, source_target_pairs={{0,2},{2,0},{4,6},{6,4},{8,10},{10,8},{12,14},{14,12},{1,3},{3,1},... | collective-permute-start | bytes 393224 | tf_op jit(solution)/shard_map/ppermute | solution.py:276
  7.8 10.4 %collective-permute-start.7 = (s32[2,128]{1,0:T(2,128)S(1)}, s32[2,128]{1,0:T(2,128)S(1)}, u32[]{:S(2)}, u32[]{:S(2)}) collective-permute-start(s32[2,128]{1,0:T(2,128)S(1)} %pad_add_fusion), channel_id=1, source_target_pairs={{0,2},{2,0},{4,6},{6,4},{8,10},{10,8},{12,14},{14,12},{1,3},{3,1},... | collective-permute-start | bytes 3080 | tf_op jit(solution)/shard_map/ppermute | solution.py:281
  10.1 11.9 %all-to-all-start = ((f32[8,16,8]{2,0,1:T(8,128)}), f32[8,16,8]{2,0,1:T(8,128)S(1)}, u32[]{:S(2)}, u32[]{:S(2)}) async-start(f32[8,16,8]{2,0,1:T(8,128)} %copy.52), calls=%async_computation | async-start | bytes 131072 | tf_op jit(solution)/shard_map/all_to_all | solution.py:278
  15.1 1.0 copy-start.5
  16.1 0.7 copy-start.10
  22.1 3.7 %collective-permute-start.6 = (f32[8,128]{1,0:T(8,128)S(1)}, f32[8,128]{1,0:T(8,128)S(1)}, u32[]{:S(2)}, u32[]{:S(2)}) collective-permute-start(f32[8,128]{1,0:T(8,128)S(1)} %all_to_all.13), channel_id=1, source_target_pairs={{0,2},{2,0},{4,6},{6,4},{8,10},{10,8},{12,14},{14,12},{1,3},{3,1},... | collective-permute-start | bytes 12296 | tf_op jit(solution)/shard_map/ppermute | solution.py:282
  25.8 5.9 %collective-permute-start.5 = (f32[16,8,256]{2,1,0:T(8,128)S(1)}, f32[16,8,256]{2,1,0:T(8,128)S(1)}, u32[]{:S(2)}, u32[]{:S(2)}) collective-permute-start(f32[16,8,256]{2,1,0:T(8,128)S(1)} %get-tuple-element.29), channel_id=1, source_target_pairs={{0,2},{2,0},{4,6},{6,4},{8,10},{10,8},{12,14},{14,12},{1,3},{3,1},... | collective-permute-start | bytes 393224 | tf_op jit(solution)/shard_map/ppermute | solution.py:276
  26.9 5.8 %collective-permute-start = (f32[16,8,256]{2,1,0:T(8,128)S(1)}, f32[16,8,256]{2,1,0:T(8,128)S(1)}, u32[]{:S(2)}, u32[]{:S(2)}) collective-permute-start(f32[16,8,256]{2,1,0:T(8,128)S(1)} %get-tuple-element.39), channel_id=1, source_target_pairs={{0,2},{2,0},{4,6},{6,4},{8,10},{10,8},{12,14},{14,12},{1,3},{3,1},... | collective-permute-start | bytes 393224 | tf_op jit(solution)/shard_map/ppermute | solution.py:276
  98.6 2.0 %copy-start = (f32[16,16,256]{2,1,0:T(8,128)S(1)}, f32[16,16,256]{2,1,0:T(8,128)}, u32[]{:S(2)}) copy-start(f32[16,16,256]{2,1,0:T(8,128)} %get-tuple-element.6) | copy-start | bytes 786436
  99.7 8.3 %collective-permute-start.9 = (f32[16,8,256]{2,1,0:T(8,128)S(1)}, f32[16,8,256]{2,1,0:T(8,128)S(1)}, u32[]{:S(2)}, u32[]{:S(2)}) collective-permute-start(f32[16,8,256]{2,1,0:T(8,128)S(1)} %get-tuple-element.25), channel_id=1, source_target_pairs={{0,2},{2,0},{4,6},{6,4},{8,10},{10,8},{12,14},{14,12},{1,3},{3,1},... | collective-permute-start | bytes 393224 | tf_op jit(solution)/shard_map/ppermute | solution.py:335
  102.2 3.6 %copy-start.6 = (f32[16,16,256]{2,1,0:T(8,128)S(1)}, f32[16,16,256]{2,1,0:T(8,128)}, u32[]{:S(2)}) copy-start(f32[16,16,256]{2,1,0:T(8,128)} %get-tuple-element.7) | copy-start | bytes 786436
  102.2 11.8 %all-to-all-start.1 = ((f32[8,1,8192]{2,1,0:T(1,128)}), f32[8,1,8192]{2,1,0:T(1,128)S(1)}, u32[]{:S(2)}, u32[]{:S(2)}) async-start(f32[8,1,8192]{2,1,0:T(1,128)} %reshape.298), calls=%async_computation.1 | async-start | bytes 524288 | tf_op jit(solution)/shard_map/all_to_all | solution.py:341
  105.9 6.1 %collective-permute-start.8 = (f32[16,8,256]{2,1,0:T(8,128)S(1)}, f32[16,8,256]{2,1,0:T(8,128)S(1)}, u32[]{:S(2)}, u32[]{:S(2)}) collective-permute-start(f32[16,8,256]{2,1,0:T(8,128)S(1)} %get-tuple-element.27), channel_id=1, source_target_pairs={{0,2},{2,0},{4,6},{6,4},{8,10},{10,8},{12,14},{14,12},{1,3},{3,1},... | collective-permute-start | bytes 393224 | tf_op jit(solution)/shard_map/ppermute | solution.py:335

commit v2 on v1

--- a/solution.py
+++ b/solution.py
@@ -34,7 +34,7 @@
     raw_out, last_out, previous_out,
     field, x_in, x_out, accel, base, image, slopes, speed_sq,
     row_map, row_map_t, z_map, z_high, z_low, residual_ref,
-    send_sem, recv_sem,
+    landing, send_sem, recv_sem, swap_send, swap_recv,
 ):
     n_i, n_x, depth, steps, n_xline, n_inline = sizes
     rows = n_i * n_x
@@ -101,6 +101,17 @@
         field[idx, field_rows, pl.ds(4, 4), :] = x_in[idx, 0, part_rows]
         field[idx, field_rows, pl.ds(8 + n_x, 4), :] = x_in[idx, 1, part_rows]
 
+    tile_x = n_x // 2
+    own_x = pl.ds(pl.multiple_of(8 + tile_x * side, 8), tile_x)
+    mate_x = pl.ds(pl.multiple_of(8 + tile_x * (1 - side), 8), tile_x)
+
+    def swap_of(which, idx):
+        return pltpu.make_async_remote_copy(
+            src_ref=field.at[idx, pl.ds(4, n_i), mate_x, :], dst_ref=landing.at[which],
+            send_sem=swap_send.at[which], recv_sem=swap_recv.at[which],
+            device_id={"xline": mate}, device_id_type=MESH,
+        )
+
     for idx in range(5):
         field[idx, pl.ds(0, 4)] = jnp.zeros((4,) + field.shape[2:], jnp.float32)
         field[idx, pl.ds(n_i + 4, 4)] = jnp.zeros((4,) + field.shape[2:], jnp.float32)
@@ -224,6 +235,11 @@
         now = 2 + lax.rem(j, 2)
         other = 5 - now
         t = steps - 1 - j
+
+        @pl.when(j == steps - 1)
+        def _():
+            swap_of(1, now).start()
+
         high, low = split_bf16(residual_ref[t] * z_map[...])
         prepare(now, dot(row_map[...], high) + dot(row_map[...], low))
 
@@ -242,9 +258,16 @@
             def _():
                 send(other, part)
 
+    final = 2 + steps % 2
+    swap_of(0, final).start()
     raw_out[...] = image[...] * (2.0 / steps) / velocity[...]
-    last_out[...] = field[2 + steps % 2, inner_i, inner_x, :]
-    previous_out[...] = field[2 + (steps - 1) % 2, inner_i, inner_x, :]
+    own_rows, mate_rows = pl.ds(half * n_i, n_i), pl.ds((1 - half) * n_i, n_i)
+    last_out[own_rows] = field[final, inner_i, own_x, :]
+    previous_out[own_rows] = field[5 - final, inner_i, own_x, :]
+    swap_of(1, 5 - final).wait()
+    previous_out[mate_rows] = landing[1]
+    swap_of(0, final).wait()
+    last_out[mate_rows] = landing[0]
 
 
 def per_device(
@@ -298,7 +321,7 @@
     kernel = functools.partial(wave_kernel, (n_i, n_x, depth, steps, n_xline, n_inline))
     raw, last, previous = pl.pallas_call(
         kernel,
-        out_shape=[jax.ShapeDtypeStruct(block, jnp.float32)] * 3,
+        out_shape=[jax.ShapeDtypeStruct(shape, jnp.float32) for shape in (block, fwd_now.shape, fwd_now.shape)],
         in_specs=[vmem] * 14,
         out_specs=[vmem] * 3,
         scratch_shapes=[
@@ -316,8 +339,11 @@
             pltpu.VMEM((depth, 2 * depth), jnp.bfloat16),
             pltpu.VMEM((depth, 2 * depth), jnp.bfloat16),
             pltpu.VMEM((steps, slots, 1), jnp.float32),
+            pltpu.VMEM((2, n_i, tile_x, depth), jnp.float32),
             pltpu.SemaphoreType.DMA((5, 6)),
             pltpu.SemaphoreType.DMA((5, 6)),
+            pltpu.SemaphoreType.DMA((2,)),
+            pltpu.SemaphoreType.DMA((2,)),
         ],
         compiler_params=pltpu.CompilerParams(
             collective_id=0, has_side_effects=True, vmem_limit_bytes=56 * 1024 * 1024
@@ -328,14 +354,6 @@
         traces, rec_row[:, None], rec_row[None, :], rec_z[:, None],
         lists[1].astype(jnp.float32)[:, None], src_row[None, :], src_z[:, None], wavelet,
     )
-
-    def split_pair(value):
-        kept = lax.dynamic_slice_in_dim(value, side * tile_x, tile_x, axis=1)
-        sent = lax.dynamic_slice_in_dim(value, (1 - side) * tile_x, tile_x, axis=1)
-        got = lax.ppermute(sent, "xline", swap)
-        return jnp.where(
-            half == 0, jnp.concatenate([kept, got], axis=0), jnp.concatenate([got, kept], axis=0)
-        )
 
     pieces = n_xline
     columns = lax.all_to_all(
@@ -350,7 +368,7 @@
         "phixz,ypx->zhiy", columns, weights.reshape(full_x, n_xline // 2, n_x),
         precision=lax.Precision.HIGHEST,
     ).reshape(depth // pieces, tile_i, full_x)
-    return gradient, split_pair(last), split_pair(previous)
+    return gradient, last, previous
 
 
 def solution(mesh):

time: 120 us -> 129 us (1.075)
  waiting for transfers between devices: 9.72 us -> 15.1 us
  Pallas kernels: 65.1 us -> 69.7 us
  other arithmetic: 10.3 us -> 8.83 us
    all_to_all x1, waiting for transfers between devices: 1.37 us -> 8.02 us  [per_device(): lax.all_to_all(raw.reshape(n_i, n_x, pieces, depth // pieces).transpose(2...]
    ppermute x1, waiting for transfers between devices: 0.01 us -> 5.92 us  [per_device(): lists = pair_up(lists, lax.ppermute(lists, 'xline', swap), 1)]
    pallas_call x1, Pallas kernels: 65.1 us -> 69.7 us  [per_device(): pl.pallas_call(kernel, out_shape=[jax.ShapeDtypeStruct(shape, jnp.float32...]
    ppermute x2 -> x0, waiting for transfers between devices: 3.31 us -> none  [split_pair(): got = lax.ppermute(sent, 'xline', swap)]
    ppermute x2 -> x0, starting transfers between devices: 3 us -> none  [split_pair(): got = lax.ppermute(sent, 'xline', swap)]
    all_to_all x1, waiting for transfers between devices: 2.99 us -> 0.01 us  [per_device(): lax.all_to_all(observed, ('xline', 'inline'), split_axis=1, concat_axis=1...]
    all_to_all x1, starting transfers between devices: 4.98 us -> 7.39 us  [per_device(): lax.all_to_all(observed, ('xline', 'inline'), split_axis=1, concat_axis=1...]
    select_n x2 -> x0, other arithmetic: 1.45 us -> none  [split_pair(): jnp.where(half == 0, jnp.concatenate([kept, got], axis=0), jnp.concatenat...]
  transfers between devices with their start and end apart: 12 -> 10, of which waited for: 5 -> 4; matrix products, arithmetic and copies ran while one was open for 11% -> 7% of each run, Pallas kernels for 0% -> 0%
where the time goes in v2:
time: 129 us
  Pallas kernels  69.7 us (54%)
  starting transfers between devices  21.2 us (16%)
  waiting for transfers between devices  15.1 us (12%)
  local copies, waits for them, and re-layouts  11.2 us (9%)
  other arithmetic  8.83 us (7%)
  matrix products  1.84 us (1%)
    pallas_call x1, Pallas kernels, per_device(): pl.pallas_call(kernel, out_shape=[jax.ShapeDtypeStruct(shape, jnp.float32...  69.7 us
    all_to_all x1, waiting for transfers between devices, per_device(): lax.all_to_all(raw.reshape(n_i, n_x, pieces, depth // pieces).transpose(2...  8.02 us
    all_to_all x1, starting transfers between devices, per_device(): lax.all_to_all(observed, ('xline', 'inline'), split_axis=1, concat_axis=1...  7.39 us
    ppermute x6, starting transfers between devices, gather_pair(): return pair_up(kept, lax.ppermute(sent, 'xline', swap), 1)  7.02 us
    ppermute x1, waiting for transfers between devices, per_device(): lists = pair_up(lists, lax.ppermute(lists, 'xline', swap), 1)  5.92 us
    unnamed x27, local copies, waits for them, and re-layouts  5.64 us
    select_n x7, other arithmetic, pair_up(): jnp.where(side == 0, jnp.concatenate([mine, theirs], axis=axis), jnp.conc...  4.37 us
    all_to_all x1, starting transfers between devices, per_device(): lax.all_to_all(raw.reshape(n_i, n_x, pieces, depth // pieces).transpose(2...  4.16 us
  transfers between devices with their start and end apart: 10, of which 4 were waited for; matrix products, arithmetic and copies ran while one was open for 7% of the time, Pallas kernels for 0%

profile of v2, /device:TPU:0, one launch (start us, length us, event | category | flops | bytes accessed | tf_op | source)
XLA Modules:
  0.0 128.8 jit_solution(6826868618879766131)
XLA Ops:
  0.6 0.8 all_to_all.11
  2.1 7.4 %all-to-all-start = ((f32[8,16,8]{2,0,1:T(8,128)}), f32[8,16,8]{2,0,1:T(8,128)S(1)}, u32[]{:S(2)}, u32[]{:S(2)}) async-start(f32[8,16,8]{2,0,1:T(8,128)} %copy.52), calls=%async_computation | async-start | bytes 131072 | tf_op jit(solution)/shard_map/all_to_all | solution.py:301
  9.6 1.9 %collective-permute-start.1 = (f32[16,8,256]{2,1,0:T(8,128)S(1)}, f32[16,8,256]{2,1,0:T(8,128)S(1)}, u32[]{:S(2)}, u32[]{:S(2)}) collective-permute-start(f32[16,8,256]{2,1,0:T(8,128)S(1)} %get-tuple-element.33), channel_id=1, source_target_pairs={{0,2},{2,0},{4,6},{6,4},{8,10},{10,8},{12,14},{14,12},{1,3},{3,1},... | collective-permute-start | bytes 393224 | tf_op jit(solution)/shard_map/ppermute | solution.py:299
  11.6 0.9 collective-permute-start.2
  12.5 1.3 collective-permute-start.3
  13.8 0.9 collective-permute-start.4
  15.5 1.2 collective-permute-start.7
  18.7 5.9 %collective-permute-done.7 = s32[2,128]{1,0:T(2,128)S(1)} collective-permute-done((s32[2,128]{1,0:T(2,128)S(1)}, s32[2,128]{1,0:T(2,128)S(1)}, u32[]{:S(2)}, u32[]{:S(2)}) %collective-permute-start.7) | collective-permute-done | bytes 1056 | tf_op jit(solution)/shard_map/ppermute | solution.py:304
  25.5 1.5 %collective-permute-start.6 = (f32[8,128]{1,0:T(8,128)S(1)}, f32[8,128]{1,0:T(8,128)S(1)}, u32[]{:S(2)}, u32[]{:S(2)}) collective-permute-start(f32[8,128]{1,0:T(8,128)S(1)} %all_to_all.13), channel_id=1, source_target_pairs={{0,2},{2,0},{4,6},{6,4},{8,10},{10,8},{12,14},{14,12},{1,3},{3,1},... | collective-permute-start | bytes 12296 | tf_op jit(solution)/shard_map/ppermute | solution.py:305
  27.0 0.9 add_select_fusion
  27.9 0.8 copy.60.rec_live
  29.2 1.4 %collective-permute-start.5 = (f32[16,8,256]{2,1,0:T(8,128)S(1)}, f32[16,8,256]{2,1,0:T(8,128)S(1)}, u32[]{:S(2)}, u32[]{:S(2)}) collective-permute-start(f32[16,8,256]{2,1,0:T(8,128)S(1)} %get-tuple-element.25), channel_id=1, source_target_pairs={{0,2},{2,0},{4,6},{6,4},{8,10},{10,8},{12,14},{14,12},{1,3},{3,1},... | collective-permute-start | bytes 393224 | tf_op jit(solution)/shard_map/ppermute | solution.py:299
  32.9 0.7 maximum_select_fusion.2.adj_now
  33.6 0.7 maximum_select_fusion.3.adj_before
  35.1 0.7 maximum_select_fusion.5.density
  36.5 0.7 maximum_select_fusion.fwd_now
  37.2 69.7 %shard_map.130 = (f32[16,16,256]{2,1,0:T(8,128)}, f32[32,8,256]{2,1,0:T(8,128)}, f32[32,8,256]{2,1,0:T(8,128)}) custom-call(f32[16,16,256]{2,1,0:T(8,128)} %maximum_select_fusion.fwd_now, f32[16,16,256]{2,1,0:T(8,128)} %maximum_select_fusion.1.fwd_before, f32[16,16,256]{2,1,0:T(8,128)} %maximum_select_fusion.2.adj_now, ...), custom_call_target="tpu_custom_call" | custom-call | tf_op jit(solution)/shard_map/pallas_call | solution.py:322
  106.9 1.2 reshape.292
  108.3 1.2 reshape.298
  109.5 4.2 %all-to-all-start.1 = ((f32[8,1,8192]{2,1,0:T(1,128)}), f32[8,1,8192]{2,1,0:T(1,128)S(1)}, u32[]{:S(2)}, u32[]{:S(2)}) async-start(f32[8,1,8192]{2,1,0:T(1,128)} %reshape.298), calls=%async_computation.1 | async-start | bytes 524288 | tf_op jit(solution)/shard_map/all_to_all | solution.py:359
  113.8 8.0 %all-to-all-done.1 = f32[8,1,8192]{2,1,0:T(1,128)S(1)} async-done(((f32[8,1,8192]{2,1,0:T(1,128)}), f32[8,1,8192]{2,1,0:T(1,128)S(1)}, u32[]{:S(2)}, u32[]{:S(2)}) %all-to-all-start.1) | async-done | bytes 262176 | tf_op jit(solution)/shard_map/all_to_all | solution.py:359
  122.4 1.3 reduce
  124.1 1.8 %fusion.8 = f32[64,2,16,32,1]{0,3,2,1,4:T(8,128)S(1)} fusion(f32[4,2,16,16,32]{4,3,2,1,0:T(8,128)S(1)} %reverse_select_fusion, f32[64]{0:T(128)S(1)} %exponential_reduce_fusion, f32[4,16]{1,0:T(4,128)S(1)} %add_convert_fusion, f32[64]{0:T(128)S(1)} %iota_convert_fusion), kind=kOutput, calls=%fused_computation.30 | convolution fusion | flops 50352128 | bytes 525056 | tf_op jit(solution)/shard_map/phixz,ypx->zhiy/dot_general | solution.py:367
  125.9 1.1 copy.64
  (63 shorter events, 11.6 us)
Async XLA Ops:
  0.6 8.9 %copy-start = (f32[32,8,256]{2,1,0:T(8,128)S(1)}, f32[32,8,256]{2,1,0:T(8,128)}, u32[]{:S(2)}) copy-start(f32[32,8,256]{2,1,0:T(8,128)} %param.12) | copy-start | bytes 786436
  2.1 23.3 %all-to-all-start = ((f32[8,16,8]{2,0,1:T(8,128)}), f32[8,16,8]{2,0,1:T(8,128)S(1)}, u32[]{:S(2)}, u32[]{:S(2)}) async-start(f32[8,16,8]{2,0,1:T(8,128)} %copy.52), calls=%async_computation | async-start | bytes 131072 | tf_op jit(solution)/shard_map/all_to_all | solution.py:301
  9.6 2.0 %copy-start.1 = (f32[32,8,256]{2,1,0:T(8,128)S(1)}, f32[32,8,256]{2,1,0:T(8,128)}, u32[]{:S(2)}) copy-start(f32[32,8,256]{2,1,0:T(8,128)} %param.13) | copy-start | bytes 786436
  9.6 2.9 %copy-start.2 = (f32[32,8,256]{2,1,0:T(8,128)S(1)}, f32[32,8,256]{2,1,0:T(8,128)}, u32[]{:S(2)}) copy-start(f32[32,8,256]{2,1,0:T(8,128)} %param.14) | copy-start | bytes 786436
  9.6 21.9 %collective-permute-start.1 = (f32[16,8,256]{2,1,0:T(8,128)S(1)}, f32[16,8,256]{2,1,0:T(8,128)S(1)}, u32[]{:S(2)}, u32[]{:S(2)}) collective-permute-start(f32[16,8,256]{2,1,0:T(8,128)S(1)} %get-tuple-element.33), channel_id=1, source_target_pairs={{0,2},{2,0},{4,6},{6,4},{8,10},{10,8},{12,14},{14,12},{1,3},{3,1},... | collective-permute-start | bytes 393224 | tf_op jit(solution)/shard_map/ppermute | solution.py:299
  11.6 2.2 %copy-start.3 = (f32[32,8,256]{2,1,0:T(8,128)S(1)}, f32[32,8,256]{2,1,0:T(8,128)}, u32[]{:S(2)}) copy-start(f32[32,8,256]{2,1,0:T(8,128)} %param.15) | copy-start | bytes 786436
  11.6 21.3 %collective-permute-start.2 = (f32[16,8,256]{2,1,0:T(8,128)S(1)}, f32[16,8,256]{2,1,0:T(8,128)S(1)}, u32[]{:S(2)}, u32[]{:S(2)}) collective-permute-start(f32[16,8,256]{2,1,0:T(8,128)S(1)} %get-tuple-element.31), channel_id=1, source_target_pairs={{0,2},{2,0},{4,6},{6,4},{8,10},{10,8},{12,14},{14,12},{1,3},{3,1},... | collective-permute-start | bytes 393224 | tf_op jit(solution)/shard_map/ppermute | solution.py:299
  12.5 4.1 %copy-start.4 = (f32[32,8,256]{2,1,0:T(8,128)S(1)}, f32[32,8,256]{2,1,0:T(8,128)}, u32[]{:S(2)}) copy-start(f32[32,8,256]{2,1,0:T(8,128)} %param.16) | copy-start | bytes 786436
  12.5 21.1 %collective-permute-start.3 = (f32[16,8,256]{2,1,0:T(8,128)S(1)}, f32[16,8,256]{2,1,0:T(8,128)S(1)}, u32[]{:S(2)}, u32[]{:S(2)}) collective-permute-start(f32[16,8,256]{2,1,0:T(8,128)S(1)} %get-tuple-element.29), channel_id=1, source_target_pairs={{0,2},{2,0},{4,6},{6,4},{8,10},{10,8},{12,14},{14,12},{1,3},{3,1},... | collective-permute-start | bytes 393224 | tf_op jit(solution)/shard_map/ppermute | solution.py:299
  13.8 0.9 copy-start.9
  13.8 20.5 %collective-permute-start.4 = (f32[16,8,256]{2,1,0:T(8,128)S(1)}, f32[16,8,256]{2,1,0:T(8,128)S(1)}, u32[]{:S(2)}, u32[]{:S(2)}) collective-permute-start(f32[16,8,256]{2,1,0:T(8,128)S(1)} %get-tuple-element.27), channel_id=1, source_target_pairs={{0,2},{2,0},{4,6},{6,4},{8,10},{10,8},{12,14},{14,12},{1,3},{3,1},... | collective-permute-start | bytes 393224 | tf_op jit(solution)/shard_map/ppermute | solution.py:299
  14.8 0.7 copy-start.8
  15.5 9.2 %collective-permute-start.7 = (s32[2,128]{1,0:T(2,128)S(1)}, s32[2,128]{1,0:T(2,128)S(1)}, u32[]{:S(2)}, u32[]{:S(2)}) collective-permute-start(s32[2,128]{1,0:T(2,128)S(1)} %pad_add_fusion), channel_id=1, source_target_pairs={{0,2},{2,0},{4,6},{6,4},{8,10},{10,8},{12,14},{14,12},{1,3},{3,1},... | collective-permute-start | bytes 3080 | tf_op jit(solution)/shard_map/ppermute | solution.py:304
  16.7 1.3 %copy-start.5 = (f32[32,8,256]{2,1,0:T(8,128)S(1)}, f32[32,8,256]{2,1,0:T(8,128)}, u32[]{:S(2)}) copy-start(f32[32,8,256]{2,1,0:T(8,128)} %param.11) | copy-start | bytes 786436
  16.7 0.7 copy-start.10
  25.5 3.7 %collective-permute-start.6 = (f32[8,128]{1,0:T(8,128)S(1)}, f32[8,128]{1,0:T(8,128)S(1)}, u32[]{:S(2)}, u32[]{:S(2)}) collective-permute-start(f32[8,128]{1,0:T(8,128)S(1)} %all_to_all.13), channel_id=1, source_target_pairs={{0,2},{2,0},{4,6},{6,4},{8,10},{10,8},{12,14},{14,12},{1,3},{3,1},... | collective-permute-start | bytes 12296 | tf_op jit(solution)/shard_map/ppermute | solution.py:305
  29.2 5.9 %collective-permute-start.5 = (f32[16,8,256]{2,1,0:T(8,128)S(1)}, f32[16,8,256]{2,1,0:T(8,128)S(1)}, u32[]{:S(2)}, u32[]{:S(2)}) collective-permute-start(f32[16,8,256]{2,1,0:T(8,128)S(1)} %get-tuple-element.25), channel_id=1, source_target_pairs={{0,2},{2,0},{4,6},{6,4},{8,10},{10,8},{12,14},{14,12},{1,3},{3,1},... | collective-permute-start | bytes 393224 | tf_op jit(solution)/shard_map/ppermute | solution.py:299
  31.5 5.0 %collective-permute-start = (f32[16,8,256]{2,1,0:T(8,128)S(1)}, f32[16,8,256]{2,1,0:T(8,128)S(1)}, u32[]{:S(2)}, u32[]{:S(2)}) collective-permute-start(f32[16,8,256]{2,1,0:T(8,128)S(1)} %get-tuple-element.35), channel_id=1, source_target_pairs={{0,2},{2,0},{4,6},{6,4},{8,10},{10,8},{12,14},{14,12},{1,3},{3,1},... | collective-permute-start | bytes 393224 | tf_op jit(solution)/shard_map/ppermute | solution.py:299
  109.5 12.4 %all-to-all-start.1 = ((f32[8,1,8192]{2,1,0:T(1,128)}), f32[8,1,8192]{2,1,0:T(1,128)S(1)}, u32[]{:S(2)}, u32[]{:S(2)}) async-start(f32[8,1,8192]{2,1,0:T(1,128)} %reshape.298), calls=%async_computation.1 | async-start | bytes 524288 | tf_op jit(solution)/shard_map/all_to_all | solution.py:359
  125.9 1.1 copy-start.7
  127.0 1.0 copy-start.6

commit v3 on v1

--- a/solution.py
+++ b/solution.py
@@ -34,7 +34,7 @@
     raw_out, last_out, previous_out,
     field, x_in, x_out, accel, base, image, slopes, speed_sq,
     row_map, row_map_t, z_map, z_high, z_low, residual_ref,
-    send_sem, recv_sem,
+    speed, send_sem, recv_sem, swap_send, swap_recv,
 ):
     n_i, n_x, depth, steps, n_xline, n_inline = sizes
     rows = n_i * n_x
@@ -114,19 +114,33 @@
     pl.semaphore_wait(barrier, sum(present.astype(jnp.int32) for present in has))
 
     inner_i = pl.ds(4, n_i)
-    field[DENSITY, inner_i, inner_x, :] = density[...]
-    field[0, inner_i, inner_x, :] = fwd_now[...]
-    send(DENSITY, 0)
-    send(DENSITY, 1)
-    send(0, 0)
-    send(0, 1)
-    field[2, inner_i, inner_x, :] = adj_now[...]
-    send(2, 0)
-    send(2, 1)
-    field[1, inner_i, inner_x, :] = fwd_before[...]
-    field[3, inner_i, inner_x, :] = adj_before[...]
-
-    speed_sq[...] = velocity[...] * velocity[...]
+    tile_x = n_x // 2
+    kept, sent = pl.ds(half * n_i, n_i), pl.ds((1 - half) * n_i, n_i)
+    own_x = pl.ds(pl.multiple_of(8 + tile_x * side, 8), tile_x)
+    inputs = (fwd_now, fwd_before, adj_now, adj_before, density)
+
+    def swap_of(which):
+        if which < 5:
+            src, dst = inputs[which].at[sent], field.at[which, inner_i, own_x, :]
+        else:
+            src = velocity.at[sent]
+            dst = speed.at[:, pl.ds(pl.multiple_of(tile_x * side, 8), tile_x), :]
+        return pltpu.make_async_remote_copy(
+            src_ref=src, dst_ref=dst,
+            send_sem=swap_send.at[which], recv_sem=swap_recv.at[which],
+            device_id={"xline": mate}, device_id_type=MESH,
+        )
+
+    for which in (DENSITY, 0, 5, 1, 2, 3):
+        swap_of(which).start()
+    for which in (DENSITY, 0, 1, 2, 3):
+        field[which, inner_i, own_x, :] = inputs[which][kept]
+    speed[:, pl.ds(pl.multiple_of(tile_x * side, 8), tile_x), :] = velocity[kept]
+    for which in (DENSITY, 0):
+        swap_of(which).wait()
+        send(which, 0)
+        send(which, 1)
+
     image[...] = jnp.zeros(image.shape, jnp.float32)
     slots = rec_row.shape[0]
     row_map[...] = (lax.broadcasted_iota(jnp.int32, (rows, slots), 0) == rec_row_t[...]).astype(jnp.float32).astype(jnp.bfloat16)
@@ -179,6 +193,10 @@
         partial = term + speed_sq[...].reshape(rows, depth) * (lap - slopes[2].reshape(rows, depth) * slope)
         base[...] = partial.reshape(n_i, n_x, depth)
 
+    swap_of(5).wait()
+    speed_sq[...] = speed[...] * speed[...]
+    for which in (1, 2, 3):
+        swap_of(which).wait()
     slopes[2] = along_depth(DENSITY)[1].reshape(n_i, n_x, depth)
     finish(DENSITY, 0)
     finish(DENSITY, 1)
@@ -188,6 +206,9 @@
         _, slope_i, slope_x = across(DENSITY, i)
         slopes[0, i] = slope_i
         slopes[1, i] = slope_x
+
+    send(2, 0)
+    send(2, 1)
 
     @pl.loop(0, steps)
     def _(t):
@@ -242,7 +263,7 @@
             def _():
                 send(other, part)
 
-    raw_out[...] = image[...] * (2.0 / steps) / velocity[...]
+    raw_out[...] = image[...] * (2.0 / steps) / speed[...]
     last_out[...] = field[2 + steps % 2, inner_i, inner_x, :]
     previous_out[...] = field[2 + (steps - 1) % 2, inner_i, inner_x, :]
 
@@ -269,11 +290,6 @@
             jnp.concatenate([mine, theirs], axis=axis),
             jnp.concatenate([theirs, mine], axis=axis),
         )
-
-    def gather_pair(value):
-        kept = lax.dynamic_slice_in_dim(value, half * n_i, n_i, axis=0)
-        sent = lax.dynamic_slice_in_dim(value, (1 - half) * n_i, n_i, axis=0)
-        return pair_up(kept, lax.ppermute(sent, "xline", swap), 1)
 
     routed = lax.all_to_all(observed, ("xline", "inline"), split_axis=1, concat_axis=1, tiled=True)
     live = (jnp.arange(CAP)[None, :] < rec_counts[0][:, None]).astype(jnp.int32).reshape(1, -1)
@@ -316,15 +332,17 @@
             pltpu.VMEM((depth, 2 * depth), jnp.bfloat16),
             pltpu.VMEM((depth, 2 * depth), jnp.bfloat16),
             pltpu.VMEM((steps, slots, 1), jnp.float32),
+            pltpu.VMEM((n_i, n_x, depth), jnp.float32),
             pltpu.SemaphoreType.DMA((5, 6)),
             pltpu.SemaphoreType.DMA((5, 6)),
+            pltpu.SemaphoreType.DMA((6,)),
+            pltpu.SemaphoreType.DMA((6,)),
         ],
         compiler_params=pltpu.CompilerParams(
             collective_id=0, has_side_effects=True, vmem_limit_bytes=56 * 1024 * 1024
         ),
     )(
-        gather_pair(fwd_now), gather_pair(fwd_before), gather_pair(adj_now), gather_pair(adj_before),
-        gather_pair(velocity), gather_pair(log_density),
+        fwd_now, fwd_before, adj_now, adj_before, velocity, log_density,
         traces, rec_row[:, None], rec_row[None, :], rec_z[:, None],
         lists[1].astype(jnp.float32)[:, None], src_row[None, :], src_z[:, None], wavelet,
     )

time: 120 us -> 126 us (1.050)
  Pallas kernels: 65.1 us -> 80.7 us
  starting transfers between devices: 20.7 us -> 15.1 us
  other arithmetic: 10.3 us -> 5.84 us
  waiting for transfers between devices: 9.72 us -> 11.7 us
  local copies, waits for them, and re-layouts: 10.7 us -> 9.21 us
    pallas_call x1, Pallas kernels: 65.1 us -> 80.7 us  [per_device(): pl.pallas_call(kernel, out_shape=[jax.ShapeDtypeStruct(block, jnp.float32...]
    ppermute x6 -> x0, starting transfers between devices: 7.33 us -> none  [gather_pair(): return pair_up(kept, lax.ppermute(sent, 'xline', swap), 1)]
    select_n x7 -> x1, other arithmetic: 4.36 us -> 0.01 us  [pair_up(): jnp.where(side == 0, jnp.concatenate([mine, theirs], axis=axis), jnp.conc...]
    ppermute x2, waiting for transfers between devices: 3.31 us -> 5.91 us  [split_pair(): got = lax.ppermute(sent, 'xline', swap)]
    ppermute x1, starting transfers between devices: 1.56 us -> 2.97 us  [per_device(): lists = pair_up(lists, lax.ppermute(lists, 'xline', swap), 1)]
    all_to_all x1, waiting for transfers between devices: 1.37 us -> 0.01 us  [per_device(): lax.all_to_all(raw.reshape(n_i, n_x, pieces, depth // pieces).transpose(2...]
    unnamed x25 -> x15, local copies, waits for them, and re-layouts: 4.68 us -> 4.47 us
  transfers between devices with their start and end apart: 12 -> 6, of which waited for: 5 -> 4; matrix products, arithmetic and copies ran while one was open for 11% -> 5% of each run, Pallas kernels for 0% -> 0%
where the time goes in v3:
time: 126 us; the launch traced here: 125 us
  Pallas kernels  80.7 us (64%)
  starting transfers between devices  15.1 us (12%)
  waiting for transfers between devices  11.7 us (9%)
  local copies, waits for them, and re-layouts  9.21 us (7%)
  other arithmetic  5.84 us (5%)
  matrix products  1.84 us (1%)
    pallas_call x1, Pallas kernels, per_device(): pl.pallas_call(kernel, out_shape=[jax.ShapeDtypeStruct(block, jnp.float32...  80.7 us
    ppermute x2, waiting for transfers between devices, split_pair(): got = lax.ppermute(sent, 'xline', swap)  5.91 us
    all_to_all x1, starting transfers between devices, per_device(): lax.all_to_all(observed, ('xline', 'inline'), split_axis=1, concat_axis=1...  4.98 us
    unnamed x15, local copies, waits for them, and re-layouts  4.47 us
    all_to_all x1, waiting for transfers between devices, per_device(): lax.all_to_all(observed, ('xline', 'inline'), split_axis=1, concat_axis=1...  3.99 us
    all_to_all x1, starting transfers between devices, per_device(): lax.all_to_all(raw.reshape(n_i, n_x, pieces, depth // pieces).transpose(2...  3.94 us
    ppermute x2, starting transfers between devices, split_pair(): got = lax.ppermute(sent, 'xline', swap)  2.99 us
    ppermute x1, starting transfers between devices, per_device(): lists = pair_up(lists, lax.ppermute(lists, 'xline', swap), 1)  2.97 us
  transfers between devices with their start and end apart: 6, of which 4 were waited for; matrix products, arithmetic and copies ran while one was open for 5% of the time, Pallas kernels for 0%

profile of v3, /device:TPU:0, one launch (start us, length us, event | category | flops | bytes accessed | tf_op | source)
XLA Modules:
  0.0 125.2 jit_solution(13582101500732874946)
XLA Ops:
  0.6 0.6 copy-done.4
  2.0 3.0 %collective-permute-start.1 = (s32[2,128]{1,0:T(2,128)S(1)}, s32[2,128]{1,0:T(2,128)S(1)}, u32[]{:S(2)}, u32[]{:S(2)}) collective-permute-start(s32[2,128]{1,0:T(2,128)S(1)} %pad_add_fusion), channel_id=1, source_target_pairs={{0,2},{2,0},{4,6},{6,4},{8,10},{10,8},{12,14},{14,12},{1,3},{3,1},... | collective-permute-start | bytes 3080 | tf_op jit(solution)/shard_map/ppermute | solution.py:297
  5.1 0.7 copy.52
  5.7 5.0 %all-to-all-start = ((f32[8,16,8]{2,0,1:T(8,128)}), f32[8,16,8]{2,0,1:T(8,128)S(1)}, u32[]{:S(2)}, u32[]{:S(2)}) async-start(f32[8,16,8]{2,0,1:T(8,128)} %copy.52), calls=%async_computation | async-start | bytes 131072 | tf_op jit(solution)/shard_map/all_to_all | solution.py:294
  10.8 0.6 copy-done.5
  12.2 0.7 copy.61.src_z
  13.6 4.0 %all-to-all-done = f32[8,16,8]{2,0,1:T(8,128)S(1)} async-done(((f32[8,16,8]{2,0,1:T(8,128)}), f32[8,16,8]{2,0,1:T(8,128)S(1)}, u32[]{:S(2)}, u32[]{:S(2)}) %all-to-all-start) | async-done | bytes 4128 | tf_op jit(solution)/shard_map/all_to_all | solution.py:294
  17.9 0.9 add_select_fusion
  18.9 0.8 copy.60.rec_live
  19.6 1.8 %collective-permute-done = f32[8,128]{1,0:T(8,128)S(1)} collective-permute-done((f32[8,128]{1,0:T(8,128)S(1)}, f32[8,128]{1,0:T(8,128)S(1)}, u32[]{:S(2)}, u32[]{:S(2)}) %collective-permute-start) | collective-permute-done | bytes 4128 | tf_op jit(solution)/shard_map/ppermute | solution.py:298
  21.7 0.7 select_bitcast_fusion.traces
  22.4 80.7 %shard_map.130 = (f32[16,16,256]{2,1,0:T(8,128)}, f32[16,16,256]{2,1,0:T(8,128)}, f32[16,16,256]{2,1,0:T(8,128)}) custom-call(f32[32,8,256]{2,1,0:T(8,128)} %fwd_now.1, f32[32,8,256]{2,1,0:T(8,128)} %fwd_before.1, f32[32,8,256]{2,1,0:T(8,128)} %adj_now.1, f32[32,8,256]{2,1,0:T(8,128)} %adj_before.1, f32[32,8,256]{2,1,0:T(8,128)} %velocity.1, ...), custom_call_target="tpu_custom_call" | custom-call | tf_op jit(solution)/shard_map/pallas_call | solution.py:315
  103.0 1.2 reshape.292
  104.5 1.2 reshape.298
  105.6 3.9 %all-to-all-start.1 = ((f32[8,1,8192]{2,1,0:T(1,128)}), f32[8,1,8192]{2,1,0:T(1,128)S(1)}, u32[]{:S(2)}, u32[]{:S(2)}) async-start(f32[8,1,8192]{2,1,0:T(1,128)} %reshape.298), calls=%async_computation.1 | async-start | bytes 524288 | tf_op jit(solution)/shard_map/all_to_all | solution.py:359
  109.6 2.1 %collective-permute-start.2 = (f32[16,8,256]{2,1,0:T(8,128)S(1)}, f32[16,8,256]{2,1,0:T(8,128)S(1)}, u32[]{:S(2)}, u32[]{:S(2)}) collective-permute-start(f32[16,8,256]{2,1,0:T(8,128)S(1)} %get-tuple-element.27), channel_id=1, source_target_pairs={{0,2},{2,0},{4,6},{6,4},{8,10},{10,8},{12,14},{14,12},{1,3},{3,1},... | collective-permute-start | bytes 393224 | tf_op jit(solution)/shard_map/ppermute | solution.py:353
  111.7 0.9 collective-permute-start.3
  112.6 4.9 %collective-permute-done.2 = f32[16,8,256]{2,1,0:T(8,128)S(1)} collective-permute-done((f32[16,8,256]{2,1,0:T(8,128)S(1)}, f32[16,8,256]{2,1,0:T(8,128)S(1)}, u32[]{:S(2)}, u32[]{:S(2)}) %collective-permute-start.2) | collective-permute-done | bytes 131104 | tf_op jit(solution)/shard_map/ppermute | solution.py:353
  117.5 0.7 maximum_select_fusion
  118.3 1.0 collective-permute-done.3
  119.3 0.7 maximum_select_fusion.1
  120.5 1.3 %reduce = f32[8,8192]{1,0:T(8,128)S(1)} reduce(f32[8,1,8192]{2,1,0:T(1,128)S(1)} %all-to-all-done.1, f32[]{:T(128)} %broadcast.347), dimensions={1}, to_apply=%all_to_all.14.reduce_sub_computation | reduce | bytes 524292 | tf_op jit(solution)/shard_map/all_to_all | solution.py:359
  122.2 1.8 %fusion.8 = f32[64,2,16,32,1]{0,3,2,1,4:T(8,128)S(1)} fusion(f32[4,2,16,16,32]{4,3,2,1,0:T(8,128)S(1)} %reverse_select_fusion, f32[64]{0:T(128)S(1)} %exponential_reduce_fusion, f32[4,16]{1,0:T(4,128)S(1)} %add_convert_fusion, f32[64]{0:T(128)S(1)} %iota_convert_fusion), kind=kOutput, calls=%fused_computation.26 | convolution fusion | flops 50352128 | bytes 525056 | tf_op jit(solution)/shard_map/phixz,ypx->zhiy/dot_general | solution.py:367
  124.1 1.1 copy.64
  (35 shorter events, 4.1 us)
Async XLA Ops:
  0.6 0.7 copy-start.4
  1.4 0.7 copy-start.3
  1.4 3.6 %copy-start.2 = (f32[8,128]{1,0:T(8,128)S(1)}, f32[8,128]{1,0:T(8,128)}, u32[]{:S(2)}) copy-start(f32[8,128]{1,0:T(8,128)} %param.17) | copy-start | bytes 12292
  2.0 10.9 %collective-permute-start.1 = (s32[2,128]{1,0:T(2,128)S(1)}, s32[2,128]{1,0:T(2,128)S(1)}, u32[]{:S(2)}, u32[]{:S(2)}) collective-permute-start(s32[2,128]{1,0:T(2,128)S(1)} %pad_add_fusion), channel_id=1, source_target_pairs={{0,2},{2,0},{4,6},{6,4},{8,10},{10,8},{12,14},{14,12},{1,3},{3,1},... | collective-permute-start | bytes 3080 | tf_op jit(solution)/shard_map/ppermute | solution.py:297
  5.7 11.9 %all-to-all-start = ((f32[8,16,8]{2,0,1:T(8,128)}), f32[8,16,8]{2,0,1:T(8,128)S(1)}, u32[]{:S(2)}, u32[]{:S(2)}) async-start(f32[8,16,8]{2,0,1:T(8,128)} %copy.52), calls=%async_computation | async-start | bytes 131072 | tf_op jit(solution)/shard_map/all_to_all | solution.py:294
  10.8 0.7 copy-start.5
  17.7 3.7 %collective-permute-start = (f32[8,128]{1,0:T(8,128)S(1)}, f32[8,128]{1,0:T(8,128)S(1)}, u32[]{:S(2)}, u32[]{:S(2)}) collective-permute-start(f32[8,128]{1,0:T(8,128)S(1)} %all_to_all.13), channel_id=1, source_target_pairs={{0,2},{2,0},{4,6},{6,4},{8,10},{10,8},{12,14},{14,12},{1,3},{3,1},... | collective-permute-start | bytes 12296 | tf_op jit(solution)/shard_map/ppermute | solution.py:298
  105.6 3.9 %copy-start.1 = (f32[16,16,256]{2,1,0:T(8,128)S(1)}, f32[16,16,256]{2,1,0:T(8,128)}, u32[]{:S(2)}) copy-start(f32[16,16,256]{2,1,0:T(8,128)} %get-tuple-element.7) | copy-start | bytes 786436
  105.6 14.4 %all-to-all-start.1 = ((f32[8,1,8192]{2,1,0:T(1,128)}), f32[8,1,8192]{2,1,0:T(1,128)S(1)}, u32[]{:S(2)}, u32[]{:S(2)}) async-start(f32[8,1,8192]{2,1,0:T(1,128)} %reshape.298), calls=%async_computation.1 | async-start | bytes 524288 | tf_op jit(solution)/shard_map/all_to_all | solution.py:359
  109.6 2.1 %copy-start = (f32[16,16,256]{2,1,0:T(8,128)S(1)}, f32[16,16,256]{2,1,0:T(8,128)}, u32[]{:S(2)}) copy-start(f32[16,16,256]{2,1,0:T(8,128)} %get-tuple-element.8) | copy-start | bytes 786436
  109.6 7.9 %collective-permute-start.2 = (f32[16,8,256]{2,1,0:T(8,128)S(1)}, f32[16,8,256]{2,1,0:T(8,128)S(1)}, u32[]{:S(2)}, u32[]{:S(2)}) collective-permute-start(f32[16,8,256]{2,1,0:T(8,128)S(1)} %get-tuple-element.27), channel_id=1, source_target_pairs={{0,2},{2,0},{4,6},{6,4},{8,10},{10,8},{12,14},{14,12},{1,3},{3,1},... | collective-permute-start | bytes 393224 | tf_op jit(solution)/shard_map/ppermute | solution.py:353
  111.7 7.6 %collective-permute-start.3 = (f32[16,8,256]{2,1,0:T(8,128)S(1)}, f32[16,8,256]{2,1,0:T(8,128)S(1)}, u32[]{:S(2)}, u32[]{:S(2)}) collective-permute-start(f32[16,8,256]{2,1,0:T(8,128)S(1)} %get-tuple-element.25), channel_id=1, source_target_pairs={{0,2},{2,0},{4,6},{6,4},{8,10},{10,8},{12,14},{14,12},{1,3},{3,1},... | collective-permute-start | bytes 393224 | tf_op jit(solution)/shard_map/ppermute | solution.py:353

commit v4 on v3

--- a/solution.py
+++ b/solution.py
@@ -131,7 +131,7 @@
             device_id={"xline": mate}, device_id_type=MESH,
         )
 
-    for which in (DENSITY, 0, 5, 1, 2, 3):
+    for which in (DENSITY, 0):
         swap_of(which).start()
     for which in (DENSITY, 0, 1, 2, 3):
         field[which, inner_i, own_x, :] = inputs[which][kept]
@@ -140,6 +140,8 @@
         swap_of(which).wait()
         send(which, 0)
         send(which, 1)
+    for which in (5, 1):
+        swap_of(which).start()
 
     image[...] = jnp.zeros(image.shape, jnp.float32)
     slots = rec_row.shape[0]
@@ -195,8 +197,6 @@
 
     swap_of(5).wait()
     speed_sq[...] = speed[...] * speed[...]
-    for which in (1, 2, 3):
-        swap_of(which).wait()
     slopes[2] = along_depth(DENSITY)[1].reshape(n_i, n_x, depth)
     finish(DENSITY, 0)
     finish(DENSITY, 1)
@@ -207,13 +207,17 @@
         slopes[0, i] = slope_i
         slopes[1, i] = slope_x
 
-    send(2, 0)
-    send(2, 1)
+    swap_of(1).wait()
 
     @pl.loop(0, steps)
     def _(t):
         now = lax.rem(t, 2)
         other = 1 - now
+        for which in (2, 3):
+            @pl.when(t == jnp.int32((which - 2) * steps // 4))
+            def _():
+                swap_of(which).start()
+
         high, low = split_bf16(src_rows * wavelet[pl.ds(t, 1), :])
         prepare(now, dot(high, src_cols) + dot(low, src_cols))
 
@@ -232,6 +236,13 @@
             @pl.when(t < steps - 1)
             def _():
                 send(other, part)
+
+        @pl.when(t == steps - 1)
+        def _():
+            swap_of(2).wait()
+            send(2, 0)
+            send(2, 1)
+            swap_of(3).wait()
 
         high, low = split_bf16(flat(other))
         picked = dot(row_map_t[...], high) + dot(row_map_t[...], low)
@@ -291,11 +302,15 @@
             jnp.concatenate([theirs, mine], axis=axis),
         )
 
-    routed = lax.all_to_all(observed, ("xline", "inline"), split_axis=1, concat_axis=1, tiled=True)
+    columns = observed.reshape(steps, n_xline // 2, 1, 2, n_inline, CAP).swapaxes(3, 4)
+    columns = jnp.broadcast_to(columns, (steps, n_xline // 2, 2, n_inline, 2, CAP))
+    routed = lax.all_to_all(
+        columns.reshape(steps, -1), ("xline", "inline"), split_axis=1, concat_axis=1, tiled=True
+    )
     live = (jnp.arange(CAP)[None, :] < rec_counts[0][:, None]).astype(jnp.int32).reshape(1, -1)
     lists = jnp.concatenate([rec_cells, live], axis=0)
     lists = pair_up(lists, lax.ppermute(lists, "xline", swap), 1)
-    traces = pair_up(routed, lax.ppermute(routed, "xline", swap), 1).T
+    traces = routed.reshape(steps, -1, 2, CAP).transpose(2, 1, 3, 0).reshape(-1, steps)
     cells = lists[0]
     slots = cells.shape[0]
     cell_i = cells // (tile_x * depth) - half * n_i

time: 126 us -> 121 us (0.960)
  waiting for transfers between devices: 11.7 us -> 7.4 us
  Pallas kernels: 80.7 us -> 78.9 us
    all_to_all x1, waiting for transfers between devices: 3.99 us -> 1.63 us  [per_device(): lax.all_to_all(columns.reshape(steps, -1), ('xline', 'inline'), split_axi...]
    ppermute x1 -> x0, waiting for transfers between devices: 1.76 us -> none  [per_device(): traces = pair_up(routed, lax.ppermute(routed, 'xline', swap), 1).T]
    pallas_call x1, Pallas kernels: 80.7 us -> 78.9 us  [per_device(): pl.pallas_call(kernel, out_shape=[jax.ShapeDtypeStruct(block, jnp.float32...]
    unnamed x15 -> x17, local copies, waits for them, and re-layouts: 4.47 us -> 5.24 us
  transfers between devices with their start and end apart: 6 -> 5, of which waited for: 4 -> 3; matrix products, arithmetic and copies ran while one was open for 5% -> 5% of each run, Pallas kernels for 0% -> 0%
where the time goes in v4:
time: 121 us
  Pallas kernels  78.9 us (65%)
  starting transfers between devices  15.5 us (13%)
  local copies, waits for them, and re-layouts  10.2 us (8%)
  waiting for transfers between devices  7.4 us (6%)
  other arithmetic  5.95 us (5%)
  matrix products  1.84 us (2%)
    pallas_call x1, Pallas kernels, per_device(): pl.pallas_call(kernel, out_shape=[jax.ShapeDtypeStruct(block, jnp.float32...  78.9 us
    ppermute x2, waiting for transfers between devices, split_pair(): got = lax.ppermute(sent, 'xline', swap)  5.76 us
    unnamed x17, local copies, waits for them, and re-layouts  5.24 us
    all_to_all x1, starting transfers between devices, per_device(): lax.all_to_all(columns.reshape(steps, -1), ('xline', 'inline'), split_axi...  4.98 us
    all_to_all x1, starting transfers between devices, per_device(): lax.all_to_all(raw.reshape(n_i, n_x, pieces, depth // pieces).transpose(2...  4.53 us
    ppermute x2, starting transfers between devices, split_pair(): got = lax.ppermute(sent, 'xline', swap)  2.99 us
    ppermute x1, starting transfers between devices, per_device(): lists = pair_up(lists, lax.ppermute(lists, 'xline', swap), 1)  2.97 us
  transfers between devices with their start and end apart: 5, of which 3 were waited for; matrix products, arithmetic and copies ran while one was open for 5% of the time, Pallas kernels for 0%

profile of v4, /device:TPU:0, one launch (start us, length us, event | category | flops | bytes accessed | tf_op | source)
XLA Modules:
  0.0 120.7 jit_solution(14491860584674573721)
XLA Ops:
  0.6 0.6 copy-done.4
  2.0 3.0 %collective-permute-start = (s32[2,128]{1,0:T(2,128)S(1)}, s32[2,128]{1,0:T(2,128)S(1)}, u32[]{:S(2)}, u32[]{:S(2)}) collective-permute-start(s32[2,128]{1,0:T(2,128)S(1)} %pad_add_fusion), channel_id=1, source_target_pairs={{0,2},{2,0},{4,6},{6,4},{8,10},{10,8},{12,14},{14,12},{1,3},{3,1},... | collective-permute-start | bytes 3080 | tf_op jit(solution)/shard_map/ppermute | solution.py:312
  5.4 0.7 reshape.313
  6.1 5.0 %all-to-all-start = ((f32[16,1,128]{2,1,0:T(1,128)}), f32[16,1,128]{2,1,0:T(1,128)S(1)}, u32[]{:S(2)}, u32[]{:S(2)}) async-start(f32[16,1,128]{2,1,0:T(1,128)} %reshape.313), calls=%async_computation | async-start | bytes 16384 | tf_op jit(solution)/shard_map/all_to_all | solution.py:307
  11.2 0.6 copy-done.5
  12.6 0.7 copy.62.src_z
  14.0 0.9 add_select_fusion
  15.0 0.8 copy.61.rec_live
  15.8 1.6 %all-to-all-done = f32[16,1,128]{2,1,0:T(1,128)S(1)} async-done(((f32[16,1,128]{2,1,0:T(1,128)}), f32[16,1,128]{2,1,0:T(1,128)S(1)}, u32[]{:S(2)}, u32[]{:S(2)}) %all-to-all-start) | async-done | bytes 8224 | tf_op jit(solution)/shard_map/all_to_all | solution.py:307
  18.0 0.7 reduce
  18.9 0.8 copy.56
  19.6 78.9 %shard_map.130 = (f32[16,16,256]{2,1,0:T(8,128)}, f32[16,16,256]{2,1,0:T(8,128)}, f32[16,16,256]{2,1,0:T(8,128)}) custom-call(f32[32,8,256]{2,1,0:T(8,128)} %fwd_now.1, f32[32,8,256]{2,1,0:T(8,128)} %fwd_before.1, f32[32,8,256]{2,1,0:T(8,128)} %adj_now.1, f32[32,8,256]{2,1,0:T(8,128)} %adj_before.1, f32[32,8,256]{2,1,0:T(8,128)} %velocity.1, ...), custom_call_target="tpu_custom_call" | custom-call | tf_op jit(solution)/shard_map/pallas_call | solution.py:330
  98.6 1.2 %reshape.307 = f32[16,16,8,32]{3,2,1,0:T(8,128)S(1)} reshape(f32[16,16,256]{2,1,0:T(8,128)} %get-tuple-element.6) | data formatting | bytes 524288 | tf_op jit(solution)/shard_map/reshape | solution.py:375
  100.0 1.2 reshape.315
  101.2 4.5 %all-to-all-start.1 = ((f32[8,1,8192]{2,1,0:T(1,128)}), f32[8,1,8192]{2,1,0:T(1,128)S(1)}, u32[]{:S(2)}, u32[]{:S(2)}) async-start(f32[8,1,8192]{2,1,0:T(1,128)} %reshape.315), calls=%async_computation.1 | async-start | bytes 524288 | tf_op jit(solution)/shard_map/all_to_all | solution.py:374
  105.7 2.1 %collective-permute-start.1 = (f32[16,8,256]{2,1,0:T(8,128)S(1)}, f32[16,8,256]{2,1,0:T(8,128)S(1)}, u32[]{:S(2)}, u32[]{:S(2)}) collective-permute-start(f32[16,8,256]{2,1,0:T(8,128)S(1)} %get-tuple-element.27), channel_id=1, source_target_pairs={{0,2},{2,0},{4,6},{6,4},{8,10},{10,8},{12,14},{14,12},{1,3},{3,1},... | collective-permute-start | bytes 393224 | tf_op jit(solution)/shard_map/ppermute | solution.py:368
  107.8 0.9 collective-permute-start.2
  108.8 4.7 %collective-permute-done.1 = f32[16,8,256]{2,1,0:T(8,128)S(1)} collective-permute-done((f32[16,8,256]{2,1,0:T(8,128)S(1)}, f32[16,8,256]{2,1,0:T(8,128)S(1)}, u32[]{:S(2)}, u32[]{:S(2)}) %collective-permute-start.1) | collective-permute-done | bytes 131104 | tf_op jit(solution)/shard_map/ppermute | solution.py:368
  113.5 0.7 maximum_select_fusion
  114.2 1.0 collective-permute-done.2
  115.2 0.7 maximum_select_fusion.1
  116.0 1.3 %reduce.1 = f32[8,8192]{1,0:T(8,128)S(1)} reduce(f32[8,1,8192]{2,1,0:T(1,128)S(1)} %all-to-all-done.1, f32[]{:T(128)} %broadcast.347), dimensions={1}, to_apply=%all_to_all.11.reduce_sub_computation | reduce | bytes 524292 | tf_op jit(solution)/shard_map/all_to_all | solution.py:374
  117.7 1.8 %fusion.8 = f32[64,2,16,32,1]{0,3,2,1,4:T(8,128)S(1)} fusion(f32[4,2,16,16,32]{4,3,2,1,0:T(8,128)S(1)} %reverse_select_fusion, f32[64]{0:T(128)S(1)} %exponential_reduce_fusion, f32[4,16]{1,0:T(4,128)S(1)} %add_convert_fusion, f32[64]{0:T(128)S(1)} %iota_convert_fusion), kind=kOutput, calls=%fused_computation.25 | convolution fusion | flops 50352128 | bytes 525056 | tf_op jit(solution)/shard_map/phixz,ypx->zhiy/dot_general | solution.py:382
  119.6 1.1 copy.65
  (35 shorter events, 4.1 us)
Async XLA Ops:
  0.6 0.7 copy-start.4
  1.4 0.7 copy-start.3
  1.4 3.6 %copy-start.2 = (f32[8,128]{1,0:T(8,128)S(1)}, f32[8,128]{1,0:T(8,128)}, u32[]{:S(2)}) copy-start(f32[8,128]{1,0:T(8,128)} %param.17) | copy-start | bytes 12292
  2.0 11.2 %collective-permute-start = (s32[2,128]{1,0:T(2,128)S(1)}, s32[2,128]{1,0:T(2,128)S(1)}, u32[]{:S(2)}, u32[]{:S(2)}) collective-permute-start(s32[2,128]{1,0:T(2,128)S(1)} %pad_add_fusion), channel_id=1, source_target_pairs={{0,2},{2,0},{4,6},{6,4},{8,10},{10,8},{12,14},{14,12},{1,3},{3,1},... | collective-permute-start | bytes 3080 | tf_op jit(solution)/shard_map/ppermute | solution.py:312
  6.1 11.3 %all-to-all-start = ((f32[16,1,128]{2,1,0:T(1,128)}), f32[16,1,128]{2,1,0:T(1,128)S(1)}, u32[]{:S(2)}, u32[]{:S(2)}) async-start(f32[16,1,128]{2,1,0:T(1,128)} %reshape.313), calls=%async_computation | async-start | bytes 16384 | tf_op jit(solution)/shard_map/all_to_all | solution.py:307
  11.1 0.7 copy-start.5
  101.2 4.5 %copy-start.1 = (f32[16,16,256]{2,1,0:T(8,128)S(1)}, f32[16,16,256]{2,1,0:T(8,128)}, u32[]{:S(2)}) copy-start(f32[16,16,256]{2,1,0:T(8,128)} %get-tuple-element.7) | copy-start | bytes 786436
  101.2 14.8 %all-to-all-start.1 = ((f32[8,1,8192]{2,1,0:T(1,128)}), f32[8,1,8192]{2,1,0:T(1,128)S(1)}, u32[]{:S(2)}, u32[]{:S(2)}) async-start(f32[8,1,8192]{2,1,0:T(1,128)} %reshape.315), calls=%async_computation.1 | async-start | bytes 524288 | tf_op jit(solution)/shard_map/all_to_all | solution.py:374
  105.7 2.1 %copy-start = (f32[16,16,256]{2,1,0:T(8,128)S(1)}, f32[16,16,256]{2,1,0:T(8,128)}, u32[]{:S(2)}) copy-start(f32[16,16,256]{2,1,0:T(8,128)} %get-tuple-element.8) | copy-start | bytes 786436
  105.7 7.7 %collective-permute-start.1 = (f32[16,8,256]{2,1,0:T(8,128)S(1)}, f32[16,8,256]{2,1,0:T(8,128)S(1)}, u32[]{:S(2)}, u32[]{:S(2)}) collective-permute-start(f32[16,8,256]{2,1,0:T(8,128)S(1)} %get-tuple-element.27), channel_id=1, source_target_pairs={{0,2},{2,0},{4,6},{6,4},{8,10},{10,8},{12,14},{14,12},{1,3},{3,1},... | collective-permute-start | bytes 393224 | tf_op jit(solution)/shard_map/ppermute | solution.py:368
  107.8 7.4 %collective-permute-start.2 = (f32[16,8,256]{2,1,0:T(8,128)S(1)}, f32[16,8,256]{2,1,0:T(8,128)S(1)}, u32[]{:S(2)}, u32[]{:S(2)}) collective-permute-start(f32[16,8,256]{2,1,0:T(8,128)S(1)} %get-tuple-element.25), channel_id=1, source_target_pairs={{0,2},{2,0},{4,6},{6,4},{8,10},{10,8},{12,14},{14,12},{1,3},{3,1},... | collective-permute-start | bytes 393224 | tf_op jit(solution)/shard_map/ppermute | solution.py:368
